TPU v7x, 32 devices: a whole 2x2x4 slice. The times are simulated.
32 devices in a mesh: groups: 2 (over y), slab: 16 (over z, x, core).
Axes of the slice: x: 2, y: 2, z: 4, core: 2. Of those that a mesh axis runs over, the one named last changes fastest.
Arguments:
- volume: bfloat16 [4096, 32, 2048], P(('groups', 'slab')), parts along dimension 0, may hold values from 0 to 2
- measured: bfloat16 [32, 512, 2048], P(('groups', 'slab')), parts along dimension 0, may hold values from 0 to 80
- path_weights: bfloat16 [16, 32], replicated, may hold values from 0.25 to 1
- fractions: float32 [16, 2048], replicated, may hold values from 0.1 to 0.5
- bases: int32 [16], replicated, may hold values from 1 to 1536, as said below
Outputs:
- new_volume: float32 [4096, 32, 2048], P(('groups', 'slab')), parts along dimension 0
There are 2 independent parts, one for each index of `groups`. A program takes and returns all parts, laid end to end along the dimension named above; an argument that names none is the same for every part. Nothing has to cross between parts.
Inputs may be any that keep to these rules, and one draw needn't show every extreme that they name: `bases`: the entries, taken in increasing order, begin with 1 and end with 1536, and consecutive ones differ by less than 512; every slice lies within, or directly before, the rows of some projection. The order of the projections along the subset is not that of the helix.
All inputs are finite; a program needn't handle non-finite values.
Results may differ from a plain program's by a relative error of at most 0.002.
Values may be sent and summed in bfloat16 or wider, within the bound.
No kernel may reach another device: no remote copies, remote signals or barrier semaphores. Data moves between devices by JAX's collectives and lax.ppermute only.
A program may use at most 192 MiB of HBM per device.

v0:
```python
import functools

import jax
import jax.numpy as jnp
from jax import lax
from jax.experimental import pallas as pl
from jax.experimental.pallas import tpu as pltpu
from jax.sharding import PartitionSpec as P

RELAX = 1.0
BLOCK = 16
HALF = 8
LANES = 128
WIDE = 256
PIECES = 4
PARTS = 2
ROUTED_CLASSES = 4
LOAD = 2
STEADY = 2
CODE = 256
LINES = 5
VMEM_LIMIT = 56 * 2**20


def dot(a, b):
    return jnp.dot(a, b, preferred_element_type=jnp.float32)


def widen(coef):
    return jnp.concatenate([coef] * (WIDE // LANES), axis=1)


def spread_out(packets):
    return [r for p in packets for r in ([p] if p.ndim == 2 else [p.at[n] for n in range(LOAD)])]


def update_kernel(
    dense, part, table_ref, lower_ref, upper_ref, next_ref, left_ref, right_ref, edge_ref, coef_ref, edge_coef_ref,
    image_w_ref, weight_ref, spread_ref, carry_w_ref, *rest,
):
    out_ref, carry_ref, seen_ref, result_ref, sems, out_sems = rest[-6:]
    packets = rest[:-7]
    block = pl.program_id(0)
    blocks = pl.num_programs(0)
    depth, width = lower_ref.shape[1:]
    angles = weight_ref.shape[0]
    first = part * blocks * BLOCK

    def fetch(at_block, act):
        slot = at_block % 2
        rows = pl.ds(pl.multiple_of(at_block * BLOCK, BLOCK), BLOCK)
        if dense:
            act(pltpu.make_async_copy(packets[0].at[:, rows], seen_ref.at[slot], sems.at[slot, 0]))
            return
        views = spread_out(packets)
        arrived = (len(views) - ROUTED_CLASSES) // 2
        names = [(4, n) for n in range(ROUTED_CLASSES)] + [(way, n) for way in (2, 3) for n in range(arrived)]
        for n, (view, (line, spot)) in enumerate(zip(views, names)):
            name = table_ref[part * LINES + line, spot]

            @pl.when(name >= 0)
            def _():
                act(pltpu.make_async_copy(view.at[rows], seen_ref.at[slot, name], sems.at[slot, n]))

    def deliver(at_block, act):
        slot = at_block % 2
        size = BLOCK // PIECES
        for n in range(PIECES):
            source = result_ref.at[slot, pl.ds(n * size, size)]
            act(pltpu.make_async_copy(source, out_ref.at[pl.ds(first + at_block * BLOCK + n * size, size)], out_sems.at[slot, n]))

    @pl.when(block == 0)
    def _():
        seen_ref[...] = jnp.zeros_like(seen_ref)
        fetch(block, lambda copy: copy.start())

    @pl.when(block + 1 < blocks)
    def _():
        fetch(block + 1, lambda copy: copy.start())

    @pl.when(block == 0)
    def _():
        if part:
            carry_ref[...] = edge_ref[...]
            return
        for chunk in range(width // WIDE):
            at = pl.ds(chunk * WIDE, WIDE)
            mine = dot(weight_ref[...], lower_ref[0, :, at])
            before = dot(weight_ref[...], left_ref[0, :, at])
            carry_ref[:, at] = (
                edge_ref[:, at].astype(jnp.float32) * widen(edge_coef_ref[2])
                - mine * widen(edge_coef_ref[0])
                - before * widen(edge_coef_ref[1])
            ).astype(jnp.bfloat16)

    @pl.when(block >= 2)
    def _():
        deliver(block - 2, lambda copy: copy.wait())

    fetch(block, lambda copy: copy.wait())
    slot = block % 2
    final = (block == blocks - 1) & (part == PARTS - 1 or dense)

    def work(chunk):
        at = pl.ds(pl.multiple_of(chunk * WIDE, WIDE), WIDE)
        seen = seen_ref[slot, :, :, at].astype(jnp.float32)
        slabs = [lower_ref[:, :, at], upper_ref[:, :, at]]
        images = [dot(image_w_ref[...], slab.reshape(HALF * depth, WIDE)) for slab in slabs]
        after = dot(weight_ref[...], jnp.where(final, right_ref[0, :, at], next_ref[0, :, at]))
        ahead = [pltpu.roll(x.reshape(angles, HALF, WIDE), HALF - 1, 1) for x in images]
        ahead.append(jnp.broadcast_to(after.reshape(angles, 1, WIDE), (angles, HALF, WIDE)))
        tail = lax.broadcasted_iota(jnp.int32, (angles, HALF, WIDE), 1) == HALF - 1
        parts = []
        for half in range(2):
            now = jnp.where(tail, ahead[half + 1], ahead[half]).reshape(angles * HALF, WIDE)
            got = seen[:, half * HALF : (half + 1) * HALF].reshape(angles * HALF, WIDE)
            coef = [widen(coef_ref[0, half, n]) for n in range(3)]
            resid = got * coef[2] - now * coef[0] - images[half] * coef[1]
            parts.append(resid.reshape(angles, HALF, WIDE))
        resid = jnp.concatenate(parts, axis=1)
        spread = dot(spread_ref[0], resid.astype(jnp.bfloat16).reshape(angles * BLOCK, WIDE))
        extra = dot(carry_w_ref[0], carry_ref[:, at])
        carry_ref[:, at] = resid[:, BLOCK - 1].astype(jnp.bfloat16)
        spread = spread.reshape(BLOCK, depth, WIDE)
        for half in range(2):
            here = slice(half * HALF, (half + 1) * HALF)
            result_ref[slot, here, :, at] = slabs[half].astype(jnp.float32) + spread[here]
        result_ref[slot, 0, :, at] += extra

    if dense:
        pl.loop(0, width // WIDE)(work)
    else:
        for chunk in range(width // WIDE):
            work(chunk)
    deliver(block, lambda copy: copy.start())

    @pl.when(block == blocks - 1)
    def _():
        @pl.when(block >= 1)
        def _():
            deliver(block - 1, lambda copy: copy.wait())

        deliver(block, lambda copy: copy.wait())


def update(volume, left, right, edge, tables, packets, table, before, part, parts, dense):
    slices, depth, cols = volume.shape
    angles = edge.shape[0]
    blocks = slices // BLOCK // parts
    off = part * blocks
    by_block = lambda x: pl.BlockSpec((1,) + x.shape[1:], lambda b, i: (b + off,) + (0,) * (x.ndim - 1))
    whole = lambda x: pl.BlockSpec(x.shape, lambda b, i: (0,) * x.ndim)
    anywhere = pl.BlockSpec(memory_space=pl.ANY)
    coef, edge_coef, image_w, weights, spread_w, carry_w = tables
    aliases = {} if before is None else {13 + len(packets): 0}
    copies = 1 if dense else ROUTED_CLASSES + LOAD * (len(packets) - ROUTED_CLASSES)
    one = (1, depth, cols)
    return pl.pallas_call(
        functools.partial(update_kernel, dense, part),
        grid_spec=pltpu.PrefetchScalarGridSpec(
            num_scalar_prefetch=1,
            grid=(blocks,),
            in_specs=[
                pl.BlockSpec((HALF, depth, cols), lambda b, i: (2 * (b + off), 0, 0)),
                pl.BlockSpec((HALF, depth, cols), lambda b, i: (2 * (b + off) + 1, 0, 0)),
                pl.BlockSpec(one, lambda b, i: (jnp.minimum((b + off + 1) * BLOCK, slices - 1), 0, 0)),
                pl.BlockSpec(one, lambda b, i: (0, 0, 0)),
                pl.BlockSpec(one, lambda b, i: (0, 0, 0)),
                whole(edge), by_block(coef), whole(edge_coef), whole(image_w), whole(weights),
                by_block(spread_w), by_block(carry_w),
            ]
            + [anywhere] * (len(packets) + 1),
            out_specs=[anywhere, whole(edge)],
            scratch_shapes=[
                pltpu.VMEM((2, angles, BLOCK, cols), jnp.bfloat16),
                pltpu.VMEM((2, BLOCK, depth, cols), jnp.float32),
                pltpu.SemaphoreType.DMA((2, copies)),
                pltpu.SemaphoreType.DMA((2, PIECES)),
            ],
        ),
        out_shape=[jax.ShapeDtypeStruct(volume.shape, jnp.float32), jax.ShapeDtypeStruct(edge.shape, edge.dtype)],
        input_output_aliases=aliases,
        compiler_params=pltpu.CompilerParams(dimension_semantics=("arbitrary",), vmem_limit_bytes=VMEM_LIMIT),
        cost_estimate=pl.CostEstimate(
            flops=4 * slices * depth * cols * angles // parts, bytes_accessed=volume.size * 7 // parts, transcendentals=0
        ),
        name="slab_update",
    )(
        table, volume, volume, volume, left, right, edge, coef, edge_coef, image_w, weights, spread_w, carry_w,
        *packets, edge if before is None else before,
    )


def fill_weights(wide_w, turned_w, pick_next, pick_now, pick_carry, spread_ref, carry_w_ref):
    depth, columns = wide_w.shape
    place = lax.broadcasted_iota(jnp.int32, (depth, columns), 1) % BLOCK
    from_next = wide_w * pick_next
    from_now = wide_w * pick_now
    from_carry = turned_w * pick_carry
    for z in range(BLOCK):
        row = jnp.where(place == z, from_next, jnp.where(place == z - 1, from_now, 0.0))
        total = jnp.sum(row, axis=1, keepdims=True)
        if z == 0:
            total = total + jnp.sum(from_carry, axis=1, keepdims=True)
            carry_w_ref[0] = (from_carry * (RELAX / total)).astype(jnp.bfloat16)
        spread_ref[0, z * depth : (z + 1) * depth] = (row * (RELAX / total)).astype(jnp.bfloat16)


def weights_kernel(wide_w_ref, turned_w_ref, pick_ref, pick_carry_ref, spread_ref, carry_w_ref):
    picks = pick_ref[0, 0:1], pick_ref[0, 1:2], pick_carry_ref[0]
    fill_weights(wide_w_ref[...], turned_w_ref[...], *picks, spread_ref, carry_w_ref)


def make_weights(wide_w, turned_w, pick, pick_carry):
    blocks = pick.shape[0]
    depth, angles = turned_w.shape
    by_block = lambda shape: pl.BlockSpec((1,) + shape, lambda b: (b,) + (0,) * len(shape))
    whole = lambda x: pl.BlockSpec(x.shape, lambda b: (0,) * x.ndim)
    spread = (BLOCK * depth, angles * BLOCK)
    carry = (depth, angles)
    return pl.pallas_call(
        weights_kernel,
        grid=(blocks,),
        in_specs=[whole(wide_w), whole(turned_w), by_block(pick.shape[1:]), by_block(pick_carry.shape[1:])],
        out_specs=[by_block(spread), by_block(carry)],
        out_shape=[
            jax.ShapeDtypeStruct((blocks,) + spread, jnp.bfloat16),
            jax.ShapeDtypeStruct((blocks,) + carry, jnp.bfloat16),
        ],
        name="spread_weights",
    )(wide_w, turned_w, pick, pick_carry)


def make_tables(share, first, rows, path_weights, bases, slices):
    angles, depth = path_weights.shape
    blocks = slices // BLOCK
    weights = path_weights.astype(jnp.float32)
    ray_total = jnp.sum(weights, axis=1)[:, None]
    norm = 1.0 / (ray_total * ((1.0 - share[:, 1:]) + share[:, :-1]))
    coefs = jnp.stack([(1.0 - share[:, 1:]) * norm, share[:, :-1] * norm, norm])
    coef = coefs[:, :, 1:].reshape(3, angles, blocks, BLOCK // HALF, HALF).transpose(2, 3, 0, 1, 4)
    coef = coef.reshape(blocks, BLOCK // HALF, 3, angles * HALF, 1)
    coef = jnp.broadcast_to(coef, coef.shape[:4] + (LANES,))
    edge_coef = jnp.broadcast_to(coefs[:, :, :1], (3, angles, LANES))
    share_own = share[:, 1:-1]
    row_now = (first - bases)[:, None] + jnp.arange(slices, dtype=jnp.int32)[None, :]
    w_now = jnp.where((row_now >= 0) & (row_now < rows), 1.0 - share_own, 0.0)
    w_next = jnp.where((row_now + 1 >= 0) & (row_now + 1 < rows), share_own, 0.0)
    pick = jnp.stack([w_next, jnp.pad(w_now[:, 1:], ((0, 0), (0, 1)))]).reshape(2, angles, blocks, BLOCK)
    pick = pick.transpose(2, 0, 1, 3).reshape(blocks, 2, angles * BLOCK)
    pick_carry = w_now[:, ::BLOCK].T[:, None, :]
    eye = jnp.eye(HALF, dtype=jnp.float32)
    image_w = jnp.einsum("ad,yz->ayzd", weights, eye).reshape(angles * HALF, HALF * depth).astype(jnp.bfloat16)
    wide_w = jnp.repeat(weights.T, BLOCK, axis=1)
    return coef, edge_coef, image_w, path_weights, *make_weights(wide_w, weights.T, pick, pick_carry)


def column_of(line, tall):
    sub = lax.broadcasted_iota(jnp.int32, (tall, LANES), 0)
    lane = lax.broadcasted_iota(jnp.int32, (tall, LANES), 1)
    return jnp.max(jnp.where(sub == lane, line, -1), axis=1, keepdims=True)


def tables_kernel(
    rows, device_ref, bases_ref, before_ref, own_ref, after_ref, weight_ref,
    coef_ref, edge_coef_ref, image_w_ref, spread_ref, carry_w_ref,
):
    block = pl.program_id(0)
    angles, depth = weight_ref.shape
    first = device_ref[0] * LANES
    shape = (angles, LANES)
    lane = lax.broadcasted_iota(jnp.int32, shape, 1)
    sub = lax.broadcasted_iota(jnp.int32, shape, 0)
    weights = weight_ref[...].astype(jnp.float32)
    ray_total = jnp.sum(weights, axis=1, keepdims=True)
    own = own_ref[...]
    ahead = jnp.where(lane == LANES - 1, pltpu.roll(after_ref[...], LANES - 1, 1), pltpu.roll(own, LANES - 1, 1))
    norm = 1.0 / (ray_total * ((1.0 - ahead) + own))
    coefs = ((1.0 - ahead) * norm, own * norm, norm)
    spots = lax.broadcasted_iota(jnp.int32, (angles, HALF, LANES), 2) - lax.broadcasted_iota(jnp.int32, (angles, HALF, LANES), 1)
    for half in range(BLOCK // HALF):
        here = spots == block * BLOCK + half * HALF
        for n, coef in enumerate(coefs):
            tall = jnp.broadcast_to(coef.reshape(angles, 1, LANES), (angles, HALF, LANES))
            tall = jnp.sum(jnp.where(here, tall, 0.0), axis=2, keepdims=True)
            coef_ref[0, half, n] = jnp.broadcast_to(tall, (angles, HALF, LANES)).reshape(angles * HALF, LANES)

    @pl.when(block == 0)
    def _():
        edge_own = jnp.sum(jnp.where(lane == 0, own, 0.0), axis=1, keepdims=True)
        edge_before = jnp.sum(jnp.where(lane == LANES - 1, before_ref[...], 0.0), axis=1, keepdims=True)
        edge_norm = 1.0 / (ray_total * ((1.0 - edge_own) + edge_before))
        for n, coef in enumerate(((1.0 - edge_own) * edge_norm, edge_before * edge_norm, edge_norm)):
            edge_coef_ref[n] = jnp.broadcast_to(coef, shape)
        across = (HALF * depth)
        repeat = lax.broadcasted_iota(jnp.int32, (depth, across), 1) % depth
        repeat = jnp.where(repeat == lax.broadcasted_iota(jnp.int32, (depth, across), 0), 1.0, 0.0)
        wide = dot(weight_ref[...], repeat.astype(jnp.bfloat16)).astype(jnp.bfloat16)
        down = angles * HALF
        expand = lax.broadcasted_iota(jnp.int32, (down, angles), 0) // HALF
        expand = jnp.where(expand == lax.broadcasted_iota(jnp.int32, (down, angles), 1), 1.0, 0.0)
        wide = dot(expand.astype(jnp.bfloat16), wide)
        at = lax.broadcasted_iota(jnp.int32, (down, across), 0) % HALF
        same = lax.broadcasted_iota(jnp.int32, (down, across), 1) // depth == at
        image_w_ref[...] = jnp.where(same, wide, 0.0).astype(jnp.bfloat16)

    row_now = first + lane - column_of(bases_ref[...], angles)
    w_now = jnp.where((row_now >= 0) & (row_now < rows), 1.0 - own, 0.0)
    w_next = jnp.where((row_now + 1 >= 0) & (row_now + 1 < rows), own, 0.0)
    columns = angles * BLOCK
    place = lax.broadcasted_iota(jnp.int32, (LANES, columns), 1) % BLOCK
    z = lax.broadcasted_iota(jnp.int32, (LANES, columns), 0) - block * BLOCK
    mine = lax.broadcasted_iota(jnp.int32, (angles, columns), 1) // BLOCK
    mine = mine == lax.broadcasted_iota(jnp.int32, (angles, columns), 0)

    def gather(values, wanted):
        picked = jnp.dot(
            values, jnp.where(wanted, 1.0, 0.0), precision=lax.Precision.HIGHEST, preferred_element_type=jnp.float32
        )
        return jnp.sum(jnp.where(mine, picked, 0.0), axis=0, keepdims=True)

    pick_next = gather(w_next, z == place)
    pick_now = gather(w_now, (z == place + 1) & (place < BLOCK - 1))
    carry = jnp.sum(jnp.where(lane == block * BLOCK, w_now, 0.0), axis=1, keepdims=True)
    square = lax.broadcasted_iota(jnp.int32, (angles, angles), 0) == lax.broadcasted_iota(jnp.int32, (angles, angles), 1)
    pick_carry = jnp.sum(jnp.where(square, carry, 0.0), axis=0, keepdims=True)
    turn = lambda other: lax.dot_general(
        weights, other, (((0,), (0,)), ((), ())), precision=lax.Precision.HIGHEST, preferred_element_type=jnp.float32
    )
    wide_w = turn(jnp.where(mine, 1.0, 0.0))
    turned_w = turn(jnp.where(square, 1.0, 0.0))
    fill_weights(wide_w, turned_w, pick_next, pick_now, pick_carry, spread_ref, carry_w_ref)


def device_tables(device, row_of_bases, fractions, path_weights, rows):
    angles, depth = path_weights.shape
    blocks = LANES // BLOCK
    last = fractions.shape[1] // LANES - 1
    column = lambda by: pl.BlockSpec((angles, LANES), lambda b, d: (0, jnp.clip(d[0] + by, 0, last)))
    whole = lambda shape: pl.BlockSpec(shape, lambda b, d: (0,) * len(shape))
    by_block = lambda shape: pl.BlockSpec((1,) + shape, lambda b, d: (b,) + (0,) * len(shape))
    coef = (BLOCK // HALF, 3, angles * HALF, LANES)
    edge_coef = (3, angles, LANES)
    image_w = (angles * HALF, HALF * depth)
    spread = (BLOCK * depth, angles * BLOCK)
    carry = (depth, angles)
    made = pl.pallas_call(
        functools.partial(tables_kernel, rows),
        grid_spec=pltpu.PrefetchScalarGridSpec(
            num_scalar_prefetch=1,
            grid=(blocks,),
            in_specs=[whole((1, LANES)), column(-1), column(0), column(1), whole(path_weights.shape)],
            out_specs=[by_block(coef), whole(edge_coef), whole(image_w), by_block(spread), by_block(carry)],
        ),
        out_shape=[
            jax.ShapeDtypeStruct((blocks,) + coef, jnp.float32),
            jax.ShapeDtypeStruct(edge_coef, jnp.float32),
            jax.ShapeDtypeStruct(image_w, jnp.bfloat16),
            jax.ShapeDtypeStruct((blocks,) + spread, jnp.bfloat16),
            jax.ShapeDtypeStruct((blocks,) + carry, jnp.bfloat16),
        ],
        name="make_tables",
    )(device, row_of_bases, fractions, fractions, fractions, path_weights)
    return made[0], made[1], made[2], path_weights, made[3], made[4]


def turn_kernel(classes, count, device_ref, bases_ref, seen_ref, *refs):
    outs, ends_ref, twice_ref, sems = refs[:-3], refs[-3], refs[-2], refs[-1]
    rows, cols = seen_ref.shape
    more = twice_ref.shape[0] - rows
    copies = [
        pltpu.make_async_copy(seen_ref, twice_ref.at[pl.ds(0, rows)], sems.at[0]),
        pltpu.make_async_copy(seen_ref.at[pl.ds(0, more)], twice_ref.at[pl.ds(rows, more)], sems.at[1]),
    ]
    for copy in copies:
        copy.start()
    for copy in copies:
        copy.wait()
    device = device_ref[0]
    base = bases_ref[device]
    my_class = device & (classes - 1)
    slices = count * PARTS

    def window(place, size, at):
        start = (place - base + 1 + rows) & (rows - 1)
        begin = pl.multiple_of(start & ~(BLOCK - 1), BLOCK)
        tall = size + BLOCK
        wide = twice_ref[pl.ds(begin, tall), at].astype(jnp.float32)
        return pltpu.roll(wide, (tall - (start - begin)) % tall, 0)

    for d in range(classes):
        for part in range(PARTS):
            out = outs[d * PARTS + part]
            place = (my_class ^ d) * slices + part * count

            @pl.loop(0, cols // WIDE)
            def _(chunk):
                at = pl.ds(pl.multiple_of(chunk * WIDE, WIDE), WIDE)
                out[:, at] = window(place, count, at)[:count].astype(jnp.bfloat16)

    @pl.loop(0, cols // WIDE)
    def _(chunk):
        at = pl.ds(pl.multiple_of(chunk * WIDE, WIDE), WIDE)
        for c in range(classes):
            ends_ref[c : c + 1, at] = window(c * slices - 1, BLOCK, at)[:1]


def turn(device, bases, seen, classes):
    rows, cols = seen.shape
    count = rows // classes // PARTS
    runs = classes * PARTS
    return pl.pallas_call(
        functools.partial(turn_kernel, classes, count),
        in_specs=[
            pl.BlockSpec(memory_space=pltpu.SMEM),
            pl.BlockSpec(memory_space=pltpu.SMEM),
            pl.BlockSpec(memory_space=pl.ANY),
        ],
        out_specs=[pl.BlockSpec(memory_space=pltpu.VMEM)] * (runs + 1),
        out_shape=[jax.ShapeDtypeStruct((count, cols), seen.dtype)] * runs + [jax.ShapeDtypeStruct((classes, cols), jnp.float32)],
        scratch_shapes=[pltpu.VMEM((rows + count + BLOCK, cols), seen.dtype), pltpu.SemaphoreType.DMA((2,))],
        compiler_params=pltpu.CompilerParams(vmem_limit_bytes=32 * 2**20),
        name="turn_rows",
    )(device, bases, seen)


def plan_kernel(slots, planes, classes, angles, count, rows, device_ref, bases_ref, table_ref):
    shape = (2 * PARTS * classes, LANES)
    lane = lax.broadcasted_iota(jnp.int32, shape, 1)
    row = lax.broadcasted_iota(jnp.int32, shape, 0)
    class_shift = classes.bit_length() - 1
    base = jnp.broadcast_to(bases_ref[...], shape) - 1
    low_plane = base >> (rows.bit_length() - 1)
    turned = base & (rows - 1)

    def reach(which):
        lowest = low_plane + jnp.where(which * count + count - 1 < turned, 1, 0)
        highest = low_plane + jnp.where(which * count < turned, 1, 0)
        return lowest, highest

    lowest, highest = reach(row >> 1)
    upward = (row & 1) == 0
    source = lane >> class_shift
    at = jnp.where(upward, source, planes - 1 - source)
    to = jnp.where(lane < angles, jnp.where(upward, highest, planes - 1 - lowest), -1)
    key = to * CODE + (CODE - 1 - lane)
    sent = [jnp.full(shape, -1, jnp.int32) for _ in range(planes - 1)]
    for slot in range(slots):
        begin = at
        for link in range(planes - 1):
            ready = (begin == link) & (to > link)
            for n in range(LOAD):
                best = jnp.max(jnp.where(ready, key, -1), axis=1, keepdims=True)
                taken = ready & (key == best)
                at = jnp.where(taken, link + 1, at)
                ready = ready & (key != best)
                which = jnp.where(best >= 0, CODE - 1 - (best & (CODE - 1)), -1)
                sent[link] = jnp.where(lane == slot * LOAD + n, which, sent[link])

    me = device_ref[0]
    my_class = me & (classes - 1)
    plane = me >> class_shift
    none = jnp.full(shape, -1, jnp.int32)
    used = none
    for link in range(planes - 1):
        used = jnp.maximum(used, sent[link])
    used = jnp.max(used, axis=0, keepdims=True)
    head = lane[:1]
    total = jnp.sum(jnp.where((used >= 0) & (head % LOAD == 0), 1, 0), axis=1, keepdims=True)

    tall = -(-max(slots * LOAD, angles) // 8) * 8
    sub = lax.broadcasted_iota(jnp.int32, (tall, LANES), 0)
    held = jnp.where(head < classes, plane * classes + (head ^ my_class), -1)
    for part in range(PARTS):
        low_here, high_here = reach(my_class * PARTS + part)
        wanted = (plane >= low_here) & (plane <= high_here) & (lane < angles)
        wanted = column_of(jnp.where(wanted, 1, 0)[:1], tall) > 0
        keep = lambda ids: jnp.max(jnp.where((sub == ids) & wanted, ids, -1), axis=0, keepdims=True)
        for way, spot in ((0, plane), (1, planes - 1 - plane)):
            sends, gets = none, none
            for link in range(planes - 1):
                sends = jnp.where(spot == link, sent[link], sends)
                gets = jnp.where(spot == link + 1, sent[link], gets)
            mine = row == 2 * (my_class * PARTS + part) + way
            sends = jnp.max(jnp.where(mine, sends, -1), axis=0, keepdims=True)
            gets = jnp.max(jnp.where(mine, gets, -1), axis=0, keepdims=True)
            arrived = jnp.max(jnp.where((column_of(gets, tall) == sends) & (sends >= 0), sub, 0), axis=0, keepdims=True)
            own = (sends >> class_shift) == plane
            index = jnp.where(own, (sends & (classes - 1)) ^ my_class, classes + arrived)
            line = part * LINES + way
            table_ref[line : line + 1] = jnp.where(sends >= 0, index, 0)
            table_ref[line + 2 : line + 3] = keep(gets)
        line = part * LINES + 4
        table_ref[line : line + 1] = keep(held)
    table_ref[PARTS * LINES : PARTS * LINES + 1] = jnp.broadcast_to(total, head.shape)


def choose_kernel(slot, part, ups, downs, table_ref, *refs):
    sources = refs[:ups], refs[ups : ups + downs]
    outs = refs[ups + downs : ups + downs + 2]
    held, sems = refs[ups + downs + 2 :]
    views = [spread_out(side) for side in sources]
    for way in range(2):
        for n in range(LOAD):
            for m, view in enumerate(views[way]):

                @pl.when(table_ref[part * LINES + way, slot * LOAD + n] == m)
                def _():
                    pltpu.make_async_copy(view, held.at[way, n], sems.at[0, way, n]).start()

    for way in range(2):
        for n in range(LOAD):
            pltpu.make_async_copy(views[way][0], held.at[way, n], sems.at[0, way, n]).wait()
            pltpu.make_async_copy(held.at[way, n], outs[way].at[n], sems.at[1, way, n]).start()
    for way in range(2):
        for n in range(LOAD):
            pltpu.make_async_copy(held.at[way, n], outs[way].at[n], sems.at[1, way, n]).wait()


def choose(slot, part, table, own, ups, downs):
    up_from, down_from = own + ups, own + downs
    anywhere = pl.BlockSpec(memory_space=pl.ANY)
    shape = jax.ShapeDtypeStruct((LOAD,) + own[0].shape, own[0].dtype)
    return pl.pallas_call(
        functools.partial(choose_kernel, slot, part, len(up_from), len(down_from)),
        in_specs=[pl.BlockSpec(memory_space=pltpu.SMEM)] + [anywhere] * (len(up_from) + len(down_from)),
        out_specs=[anywhere, anywhere],
        out_shape=[shape, shape],
        scratch_shapes=[
            pltpu.VMEM((2, LOAD) + own[0].shape, own[0].dtype),
            pltpu.SemaphoreType.DMA((2, 2, LOAD)),
        ],
        cost_estimate=pl.CostEstimate(flops=0, bytes_accessed=4 * LOAD * own[0].size * 2, transcendentals=0),
        name="choose_packet",
    )(table, *up_from, *down_from)


def on_device(volume, measured, path_weights, fractions, bases):
    slices, depth, cols = volume.shape
    local, rows = measured.shape[:2]
    nslab = lax.axis_size("slab")
    device = lax.axis_index("slab")
    angles = local * nslab
    first = device * slices
    classes = rows // slices
    planes = nslab // classes
    ups_of = lambda step: [(i, i + step) for i in range(nslab - step)]
    downs_of = lambda step: [(i + step, i) for i in range(nslab - step)]

    routed = local == 1 and classes == ROUTED_CLASSES and slices == LANES and rows & (rows - 1) == 0 and angles <= LANES
    if not routed:
        left = lax.ppermute(volume[slices - 1 :], "slab", ups_of(1))
        right = lax.ppermute(volume[:1], "slab", downs_of(1))
        share = lax.dynamic_slice_in_dim(jnp.pad(fractions, ((0, 0), (1, 1))), first, slices + 2, 1)
        tables = make_tables(share, first, rows, path_weights, bases, slices)
        my_bases = lax.dynamic_slice_in_dim(bases, device * local, local, 0)
        turned = jax.vmap(lambda m, b: jnp.roll(m, b - 1, axis=0))(measured, my_bases)
        by_class = turned.reshape(local, classes, slices, cols).transpose(1, 0, 2, 3)
        outgoing = jnp.tile(by_class, (planes, 1, 1, 1)).reshape(angles, slices, cols)
        seen = lax.all_to_all(outgoing, "slab", split_axis=0, concat_axis=0, tiled=True)
        ends = jnp.roll(by_class[:, :, slices - 1], 1, axis=0)
        ends = jnp.tile(ends, (planes, 1, 1)).reshape(angles, cols // LANES, LANES)
        edge = lax.all_to_all(ends, "slab", split_axis=0, concat_axis=0, tiled=True).reshape(angles, cols)
        return update(volume, left, right, edge, tables, [seen], jnp.zeros((8, LANES), jnp.int32), None, 0, 1, True)[0]

    number = device.astype(jnp.int32)[None]
    *runs, ends = turn(number, bases, measured[0], classes)
    row_of_bases = jnp.pad(bases, (0, LANES - angles), constant_values=1)[None]
    runs, row_of_bases = lax.optimization_barrier((runs, row_of_bases))
    own = []
    for part in range(PARTS):
        mine = [runs[d * PARTS + part] for d in range(classes)]
        if part:
            mine, own[-1] = lax.optimization_barrier((mine, own[-1]))
        own.append(
            mine[:1] + [lax.ppermute(mine[d], "slab", [(i, i ^ d) for i in range(nslab)]) for d in range(1, classes)]
        )

    most = -(-classes * (planes - 1) // LOAD) + planes - 2
    table = pl.pallas_call(
        functools.partial(plan_kernel, most, planes, classes, angles, slices // PARTS, rows),
        in_specs=[pl.BlockSpec(memory_space=pltpu.SMEM), pl.BlockSpec(memory_space=pltpu.VMEM)],
        out_shape=jax.ShapeDtypeStruct((16, LANES), jnp.int32),
        name="plan_slots",
    )(number, row_of_bases)
    slots = table[PARTS * LINES, 0]
    late = (ends, fractions, volume[slices - 1 :], volume[:1])

    def run_slots(begin, end, ups, downs):
        nonlocal late
        ups, downs = [list(u) for u in ups], [list(d) for d in downs]
        for slot in range(begin, end):
            for part in range(PARTS):
                go_up, go_down = choose(slot, part, table, own[part], ups[part], downs[part])
                if slot == 0 and part == PARTS - 1:
                    go_up, *late = lax.optimization_barrier((go_up, *late))
                ups[part].append(lax.ppermute(go_up, "slab", ups_of(classes)))
                downs[part].append(lax.ppermute(go_down, "slab", downs_of(classes)))
        return ups, downs

    ups, downs = run_slots(0, STEADY, [[] for _ in range(PARTS)], [[] for _ in range(PARTS)])
    ends, late_fractions, low, high = late
    tables = device_tables(number, row_of_bases, late_fractions, path_weights, rows)
    left = lax.ppermute(low, "slab", ups_of(1))
    right = lax.ppermute(high, "slab", downs_of(1))
    ends = jnp.tile(ends.astype(jnp.bfloat16)[None], (planes, 1, 1)).reshape(angles, cols // LANES, LANES)
    edge = lax.all_to_all(ends, "slab", split_axis=0, concat_axis=0, tiled=True).reshape(angles, cols)
    left, right, edge, tables = lax.optimization_barrier((left, right, edge, tables))

    def finish(end):
        def branch(ups, downs):
            ups, downs = run_slots(STEADY, end, ups, downs)
            out, carry = None, edge
            for part in range(PARTS):
                packets = own[part] + ups[part] + downs[part]
                out, carry = update(volume, left, right, carry, tables, packets, table, out, part, PARTS, False)
            return out

        return branch

    ends_at = [STEADY + 1, STEADY + 2, most]
    which = jnp.sum(jnp.array([slots > e for e in ends_at[:-1]]).astype(jnp.int32))
    return lax.switch(which, [finish(e) for e in ends_at], ups, downs)


def solution(mesh):
    placed = (P(("groups", "slab"), None, None), P(("groups", "slab"), None, None), P(), P(), P())
    return jax.shard_map(
        on_device,
        mesh=mesh,
        in_specs=placed,
        out_specs=P(("groups", "slab"), None, None),
        check_vma=False,
    )
```

profile of v0, /device:TPU:0, one launch (start us, length us, event | category | flops | bytes accessed | tf_op | source)
XLA Modules:
  0.0 161.3 jit_solution(1293599642014601170)
XLA Ops:
  1.2 1.6 copy-done
  3.4 3.6 %turn_rows.1 = (bf16[64,2048]{1,0:T(8,128)(2,1)S(1)}, bf16[64,2048]{1,0:T(8,128)(2,1)S(1)}, bf16[64,2048]{1,0:T(8,128)(2,1)S(1)}, bf16[64,2048]{1,0:T(8,128)(2,1...) custom-call(s32[1]{0:T(128)} %bitcast.device_ref, ...), custom_call_target="tpu_custom_call" | custom-call | tf_op jit(solution)/shard_map/turn_rows/pallas_call | solution.py:412
  7.5 2.6 %collective-permute-start.37 = (bf16[64,2048]{1,0:T(8,128)(2,1)S(1)}, bf16[64,2048]{1,0:T(8,128)(2,1)S(1)}, u32[]{:S(2)}, u32[]{:S(2)}) collective-permute-start(bf16[64,2048]{1,0:T(8,128)(2,1)S(1)} %get-tuple-element.365), channel_id=1, source_target_pairs={{0,2},{1,3},{2,0},{3,1},{4,6},{5,7},{6,4},{7,5},{8,10},{9,11},{10,... | collective-permute-start | bytes 786440 | tf_op jit(solution)/shard_map/ppermute | solution.py:576
  10.1 3.4 %plan_slots.1.table_ref = s32[16,128]{1,0:T(8,128)S(1)} custom-call(s32[1]{0:T(128)} %bitcast.device_ref, s32[1,128]{1,0:T(1,128)} %pad_bitcast_fusion.bases_ref), custom_call_target="tpu_custom_call" | custom-call | tf_op jit(solution)/shard_map/plan_slots/pallas_call | solution.py:580
  13.5 3.7 %collective-permute-done.37.refs_2_.refs_6_.refs_7_ = bf16[64,2048]{1,0:T(8,128)(2,1)S(1)} collective-permute-done((bf16[64,2048]{1,0:T(8,128)(2,1)S(1)}, bf16[64,2048]{1,0:T(8,128)(2,1)S(1)}, u32[]{:S(2)}, u32[]{:S(2)}) %collective-permute-start.37) | collective-permute-done | bytes 262176 | tf_op jit(solution)/shard_map/ppermute | solution.py:576
  17.2 5.1 %collective-permute-done.38.refs_3_.refs_7_.refs_8_ = bf16[64,2048]{1,0:T(8,128)(2,1)S(1)} collective-permute-done((bf16[64,2048]{1,0:T(8,128)(2,1)S(1)}, bf16[64,2048]{1,0:T(8,128)(2,1)S(1)}, u32[]{:S(2)}, u32[]{:S(2)}) %collective-permute-start.38) | collective-permute-done | bytes 262176 | tf_op jit(solution)/shard_map/ppermute | solution.py:576
  22.4 1.7 %collective-permute-start.44 = (bf16[64,2048]{1,0:T(8,128)(2,1)S(1)}, bf16[64,2048]{1,0:T(8,128)(2,1)S(1)}, u32[]{:S(2)}, u32[]{:S(2)}) collective-permute-start(bf16[64,2048]{1,0:T(8,128)(2,1)S(1)} %get-tuple-element.377), channel_id=1, source_target_pairs={{0,2},{1,3},{2,0},{3,1},{4,6},{5,7},{6,4},{7,5},{8,10},{9,11},{10,... | collective-permute-start | bytes 786440 | tf_op jit(solution)/shard_map/ppermute | solution.py:576
  24.2 1.7 %fusion.1 = (bf16[1,32,2048]{2,1,0:T(8,128)(2,1)}, bf16[1,32,2048]{2,1,0:T(8,128)(2,1)}) fusion(bf16[128,32,2048]{2,1,0:T(8,128)(2,1)} %param.8), kind=kLoop, calls=%fused_computation.4 | loop fusion | bytes 524288 | tf_op jit(solution)/shard_map/slice | solution.py:587
  25.9 1.9 %choose_packet.40 = (bf16[2,64,2048]{2,1,0:T(8,128)(2,1)}, bf16[2,64,2048]{2,1,0:T(8,128)(2,1)}) custom-call(s32[16,128]{1,0:T(8,128)S(1)} %plan_slots.1.table_ref, bf16[64,2048]{1,0:T(8,128)(2,1)S(1)} %get-tuple-element.367.refs_0_.refs_4_.refs_5_, bf16[64,2048]{1,0:T(8,128)(2,1)S(1)} %collective-permute-done.36.refs_1_.refs_5_.refs_6_, ...), custom_call_target="tpu_custom_call" | custom-call | bytes 2097152 | tf_op jit(solution)/shard_map/choose_packet/pallas_call | solution.py:524
  27.8 3.6 %collective-permute-start.39 = (bf16[2,64,2048]{2,1,0:T(8,128)(2,1)}, bf16[2,64,2048]{2,1,0:T(8,128)(2,1)S(1)}, u32[]{:S(2)}, u32[]{:S(2)}) collective-permute-start(bf16[2,64,2048]{2,1,0:T(8,128)(2,1)} %get-tuple-element.371), channel_id=1, source_target_pairs={{0,4},{1,5},{2,6},{3,7},{4,8},{5,9},{6,10},{7,11},{8,12},{9,13},{1... | collective-permute-start | bytes 1572872 | tf_op jit(solution)/shard_map/ppermute | solution.py:597
  31.4 1.3 collective-permute-start.40
  32.7 3.4 %collective-permute-done.45.refs_3_.refs_7_.refs_8_ = bf16[64,2048]{1,0:T(8,128)(2,1)S(1)} collective-permute-done((bf16[64,2048]{1,0:T(8,128)(2,1)S(1)}, bf16[64,2048]{1,0:T(8,128)(2,1)S(1)}, u32[]{:S(2)}, u32[]{:S(2)}) %collective-permute-start.45) | collective-permute-done | bytes 262176 | tf_op jit(solution)/shard_map/ppermute | solution.py:576
  36.1 1.9 %choose_packet.42 = (bf16[2,64,2048]{2,1,0:T(8,128)(2,1)}, bf16[2,64,2048]{2,1,0:T(8,128)(2,1)}) custom-call(s32[16,128]{1,0:T(8,128)S(1)} %plan_slots.1.table_ref, bf16[64,2048]{1,0:T(8,128)(2,1)S(1)} %get-tuple-element.375.refs_0_.refs_4_.refs_5_, bf16[64,2048]{1,0:T(8,128)(2,1)S(1)} %collective-permute-done.43.refs_1_.refs_5_.refs_6_, ...), custom_call_target="tpu_custom_call" | custom-call | bytes 2097152 | tf_op jit(solution)/shard_map/choose_packet/pallas_call | solution.py:524
  38.0 3.4 %collective-permute-start.48 = (bf16[2,64,2048]{2,1,0:T(8,128)(2,1)}, bf16[2,64,2048]{2,1,0:T(8,128)(2,1)S(1)}, u32[]{:S(2)}, u32[]{:S(2)}) collective-permute-start(bf16[2,64,2048]{2,1,0:T(8,128)(2,1)} %get-tuple-element.399), channel_id=1, source_target_pairs={{0,4},{1,5},{2,6},{3,7},{4,8},{5,9},{6,10},{7,11},{8,12},{9,13},{1... | collective-permute-start | bytes 1572872 | tf_op jit(solution)/shard_map/ppermute | solution.py:597
  43.9 4.5 %collective-permute-done.40.refs_9_ = bf16[2,64,2048]{2,1,0:T(8,128)(2,1)} collective-permute-done((bf16[2,64,2048]{2,1,0:T(8,128)(2,1)}, bf16[2,64,2048]{2,1,0:T(8,128)(2,1)}, u32[]{:S(2)}, u32[]{:S(2)}) %collective-permute-start.40) | collective-permute-done | bytes 524320 | tf_op jit(solution)/shard_map/ppermute | solution.py:598
  48.4 1.9 %choose_packet.41 = (bf16[2,64,2048]{2,1,0:T(8,128)(2,1)}, bf16[2,64,2048]{2,1,0:T(8,128)(2,1)}) custom-call(s32[16,128]{1,0:T(8,128)S(1)} %plan_slots.1.table_ref, bf16[64,2048]{1,0:T(8,128)(2,1)S(1)} %get-tuple-element.367.refs_0_.refs_4_.refs_5_, bf16[64,2048]{1,0:T(8,128)(2,1)S(1)} %collective-permute-done.36.refs_1_.refs_5_.refs_6_, ...), custom_call_target="tpu_custom_call" | custom-call | bytes 2097152 | tf_op jit(solution)/shard_map/choose_packet/pallas_call | solution.py:524
  50.3 4.3 %collective-permute-start.41 = (bf16[2,64,2048]{2,1,0:T(8,128)(2,1)}, bf16[2,64,2048]{2,1,0:T(8,128)(2,1)}, u32[]{:S(2)}, u32[]{:S(2)}) collective-permute-start(bf16[2,64,2048]{2,1,0:T(8,128)(2,1)} %get-tuple-element.373), channel_id=1, source_target_pairs={{0,4},{1,5},{2,6},{3,7},{4,8},{5,9},{6,10},{7,11},{8,12},{9,13},{1... | collective-permute-start | bytes 1572872 | tf_op jit(solution)/shard_map/ppermute | solution.py:597
  55.9 3.7 %collective-permute-done.49.refs_9_ = bf16[2,64,2048]{2,1,0:T(8,128)(2,1)} collective-permute-done((bf16[2,64,2048]{2,1,0:T(8,128)(2,1)}, bf16[2,64,2048]{2,1,0:T(8,128)(2,1)}, u32[]{:S(2)}, u32[]{:S(2)}) %collective-permute-start.49) | collective-permute-done | bytes 524320 | tf_op jit(solution)/shard_map/ppermute | solution.py:598
  59.6 2.0 %choose_packet.43 = (bf16[2,64,2048]{2,1,0:T(8,128)(2,1)}, bf16[2,64,2048]{2,1,0:T(8,128)(2,1)}) custom-call(s32[16,128]{1,0:T(8,128)S(1)} %plan_slots.1.table_ref, bf16[64,2048]{1,0:T(8,128)(2,1)S(1)} %get-tuple-element.375.refs_0_.refs_4_.refs_5_, bf16[64,2048]{1,0:T(8,128)(2,1)S(1)} %collective-permute-done.43.refs_1_.refs_5_.refs_6_, ...), custom_call_target="tpu_custom_call" | custom-call | bytes 2097152 | tf_op jit(solution)/shard_map/choose_packet/pallas_call | solution.py:524
  61.6 4.3 %collective-permute-start.50 = (bf16[2,64,2048]{2,1,0:T(8,128)(2,1)}, bf16[2,64,2048]{2,1,0:T(8,128)(2,1)}, u32[]{:S(2)}, u32[]{:S(2)}) collective-permute-start(bf16[2,64,2048]{2,1,0:T(8,128)(2,1)} %get-tuple-element.401), channel_id=1, source_target_pairs={{0,4},{1,5},{2,6},{3,7},{4,8},{5,9},{6,10},{7,11},{8,12},{9,13},{1... | collective-permute-start | bytes 1572872 | tf_op jit(solution)/shard_map/ppermute | solution.py:597
  67.2 1.3 collective-permute-start.46
  71.6 16.6 %all-to-all-start = ((bf16[16,16,128]{2,1,0:T(8,128)(2,1)}), bf16[16,16,128]{2,1,0:T(8,128)(2,1)S(1)}, u32[]{:S(2)}, u32[]{:S(2)}) async-start(bf16[16,16,128]{2,1,0:T(8,128)(2,1)} %tile.8), calls=%async_computation | async-start | bytes 131072 | tf_op jit(solution)/shard_map/all_to_all | solution.py:607
  91.6 8.9 %make_tables.1 = (f32[8,2,3,128,128]{4,3,2,1,0:T(8,128)}, f32[3,16,128]{2,1,0:T(8,128)S(1)}, bf16[128,256]{1,0:T(8,128)(2,1)}, bf16[8,512,256]{2,1,0:T(8,128)(2,1)}, bf16[8,32,16]{2,1,0:T(8,128)(2,1)}) custom-call(s32[1]{0:T(128)} %bitcast.device_ref, s32[1,128]{1,0:T(1,128)} %pad_bitcast_fusion.bases_ref, f32[16,2048]{1,0:T(8,128)} %after_ref, ...), custom_call_target="tpu_custom_call" | custom-call | tf_op jit(solution)/shard_map/make_tables/pallas_call | solution.py:347
  102.0 59.0 %conditional.1 = (f32[128,32,2048]{2,1,0:T(8,128)}) conditional(s32[]{:T(128)} %clamp.3, (s32[16,128]{1,0:T(8,128)S(1)}, bf16[64,2048]{1,0:T(8,128)(2,1)S(1)}, bf16[64,2048]{1,0:T(8,128)(2,1)S(1)}, bf16[64,2048]{1,0:T(8,128)(2,1)S(1)}, bf16[64,2048]{1,0:T(8,128)(2,1)S(1)}, /*index=5*/bf16[2,64,2048]{2,1,0:T(8,128)(2,1)S(1)}, ...), branch_computations={%region_1.2_spmd, %region_2.3_spmd, %region_3.4_spmd} | conditional | flops 536870912 | bytes 151295072 | solution.py:623
  102.1 1.9 %choose_packet.22 = (bf16[2,64,2048]{2,1,0:T(8,128)(2,1)}, bf16[2,64,2048]{2,1,0:T(8,128)(2,1)}) custom-call(s32[16,128]{1,0:T(8,128)S(1)} %get-tuple-element.170.table_ref, bf16[64,2048]{1,0:T(8,128)(2,1)S(1)} %get-tuple-element.182.refs_0_.refs_6_.rest_0_, bf16[64,2048]{1,0:T(8,128)(2,1)S(1)} %get-tuple-element.183.refs_1_.refs_7_.rest_1_, ...), custom_call_target="tpu_custom_call" | custom-call | bytes 2097152 | tf_op jit(solution)/shard_map/cond/branch_0_fun/choose_packet/pallas_call | solution.py:524
  104.0 5.4 %collective-permute-start = (bf16[2,64,2048]{2,1,0:T(8,128)(2,1)}, bf16[2,64,2048]{2,1,0:T(8,128)(2,1)}, u32[]{:S(2)}, u32[]{:S(2)}) collective-permute-start(bf16[2,64,2048]{2,1,0:T(8,128)(2,1)} %get-tuple-element.190), channel_id=1, source_target_pairs={{0,4},{1,5},{2,6},{3,7},{4,8},{5,9},{6,10},{7,11},{8,12},{9,13},{1... | collective-permute-start | bytes 1572872 | tf_op jit(solution)/shard_map/cond/branch_0_fun/ppermute | solution.py:597
  110.7 1.9 %choose_packet.23 = (bf16[2,64,2048]{2,1,0:T(8,128)(2,1)}, bf16[2,64,2048]{2,1,0:T(8,128)(2,1)}) custom-call(s32[16,128]{1,0:T(8,128)S(1)} %get-tuple-element.170.table_ref, bf16[64,2048]{1,0:T(8,128)(2,1)S(1)} %get-tuple-element.193.refs_0_.refs_6_.rest_0_, bf16[64,2048]{1,0:T(8,128)(2,1)S(1)} %get-tuple-element.194.refs_1_.refs_7_.rest_1_, ...), custom_call_target="tpu_custom_call" | custom-call | bytes 2097152 | tf_op jit(solution)/shard_map/cond/branch_0_fun/choose_packet/pallas_call | solution.py:524
  112.6 5.6 %collective-permute-start.2 = (bf16[2,64,2048]{2,1,0:T(8,128)(2,1)}, bf16[2,64,2048]{2,1,0:T(8,128)(2,1)S(1)}, u32[]{:S(2)}, u32[]{:S(2)}) collective-permute-start(bf16[2,64,2048]{2,1,0:T(8,128)(2,1)} %get-tuple-element.201), channel_id=1, source_target_pairs={{0,4},{1,5},{2,6},{3,7},{4,8},{5,9},{6,10},{7,11},{8,12},{9,13},{1... | collective-permute-start | bytes 1572872 | tf_op jit(solution)/shard_map/cond/branch_0_fun/ppermute | solution.py:597
  119.6 1.6 collective-permute-done.rest_6_
  121.2 5.2 %collective-permute-done.1.rest_9_ = bf16[2,64,2048]{2,1,0:T(8,128)(2,1)} collective-permute-done((bf16[2,64,2048]{2,1,0:T(8,128)(2,1)}, bf16[2,64,2048]{2,1,0:T(8,128)(2,1)}, u32[]{:S(2)}, u32[]{:S(2)}) %collective-permute-start.1) | collective-permute-done | bytes 524320 | tf_op jit(solution)/shard_map/cond/branch_0_fun/ppermute | solution.py:598
  126.4 16.9 %slab_update.6 = (f32[128,32,2048]{2,1,0:T(8,128)}, bf16[16,2048]{1,0:T(8,128)(2,1)}) custom-call(s32[16,128]{1,0:T(8,128)S(1)} %get-tuple-element.170.table_ref, bf16[128,32,2048]{2,1,0:T(8,128)(2,1)} %get-tuple-element.172.lower_ref.upper_ref.next_ref, bf16[128,32,2048]{2,1,0:T(8,128)(2,1)} %get-tuple-element.172.lower_ref.upper_ref.next_ref, ...), custom_call_target="tpu_custom_call" | custom-call | flops 268435456 | bytes 29360128 | tf_op jit(solution)/shard_map/cond/branch_0_fun/slab_update/pallas_call | solution.py:158
  144.3 16.4 %slab_update.7 = (f32[128,32,2048]{2,1,0:T(8,128)}, bf16[16,2048]{1,0:T(8,128)(2,1)}) custom-call(s32[16,128]{1,0:T(8,128)S(1)} %get-tuple-element.170.table_ref, bf16[128,32,2048]{2,1,0:T(8,128)(2,1)} %get-tuple-element.172.lower_ref.upper_ref.next_ref, ...), custom_call_target="tpu_custom_call", output_to_operand_aliasing={{0}: (23, {})} | custom-call | flops 268435456 | bytes 29360128 | tf_op jit(solution)/shard_map/cond/branch_0_fun/slab_update/pallas_call | solution.py:158
  (44 shorter events, 17.1 us)
Async XLA Ops:
  1.2 1.6 copy-start
  2.7 0.7 copy-start.1
  7.0 6.5 %collective-permute-start.36 = (bf16[64,2048]{1,0:T(8,128)(2,1)S(1)}, bf16[64,2048]{1,0:T(8,128)(2,1)S(1)}, u32[]{:S(2)}, u32[]{:S(2)}) collective-permute-start(bf16[64,2048]{1,0:T(8,128)(2,1)S(1)} %get-tuple-element.364), channel_id=1, source_target_pairs={{0,1},{1,0},{2,3},{3,2},{4,5},{5,4},{6,7},{7,6},{8,9},{9,8},{10,11... | collective-permute-start | bytes 786440 | tf_op jit(solution)/shard_map/ppermute | solution.py:576
  7.5 9.7 %collective-permute-start.37 = (bf16[64,2048]{1,0:T(8,128)(2,1)S(1)}, bf16[64,2048]{1,0:T(8,128)(2,1)S(1)}, u32[]{:S(2)}, u32[]{:S(2)}) collective-permute-start(bf16[64,2048]{1,0:T(8,128)(2,1)S(1)} %get-tuple-element.365), channel_id=1, source_target_pairs={{0,2},{1,3},{2,0},{3,1},{4,6},{5,7},{6,4},{7,5},{8,10},{9,11},{10,... | collective-permute-start | bytes 786440 | tf_op jit(solution)/shard_map/ppermute | solution.py:576
  10.1 12.3 %collective-permute-start.38 = (bf16[64,2048]{1,0:T(8,128)(2,1)S(1)}, bf16[64,2048]{1,0:T(8,128)(2,1)S(1)}, u32[]{:S(2)}, u32[]{:S(2)}) collective-permute-start(bf16[64,2048]{1,0:T(8,128)(2,1)S(1)} %get-tuple-element.366), channel_id=1, source_target_pairs={{0,3},{1,2},{2,1},{3,0},{4,7},{5,6},{6,5},{7,4},{8,11},{9,10},{10,... | collective-permute-start | bytes 786440 | tf_op jit(solution)/shard_map/ppermute | solution.py:576
  22.3 10.4 %collective-permute-start.43 = (bf16[64,2048]{1,0:T(8,128)(2,1)S(1)}, bf16[64,2048]{1,0:T(8,128)(2,1)S(1)}, u32[]{:S(2)}, u32[]{:S(2)}) collective-permute-start(bf16[64,2048]{1,0:T(8,128)(2,1)S(1)} %get-tuple-element.376), channel_id=1, source_target_pairs={{0,1},{1,0},{2,3},{3,2},{4,5},{5,4},{6,7},{7,6},{8,9},{9,8},{10,11... | collective-permute-start | bytes 786440 | tf_op jit(solution)/shard_map/ppermute | solution.py:576
  22.4 10.3 %collective-permute-start.44 = (bf16[64,2048]{1,0:T(8,128)(2,1)S(1)}, bf16[64,2048]{1,0:T(8,128)(2,1)S(1)}, u32[]{:S(2)}, u32[]{:S(2)}) collective-permute-start(bf16[64,2048]{1,0:T(8,128)(2,1)S(1)} %get-tuple-element.377), channel_id=1, source_target_pairs={{0,2},{1,3},{2,0},{3,1},{4,6},{5,7},{6,4},{7,5},{8,10},{9,11},{10,... | collective-permute-start | bytes 786440 | tf_op jit(solution)/shard_map/ppermute | solution.py:576
  24.2 11.9 %collective-permute-start.45 = (bf16[64,2048]{1,0:T(8,128)(2,1)S(1)}, bf16[64,2048]{1,0:T(8,128)(2,1)S(1)}, u32[]{:S(2)}, u32[]{:S(2)}) collective-permute-start(bf16[64,2048]{1,0:T(8,128)(2,1)S(1)} %get-tuple-element.378), channel_id=1, source_target_pairs={{0,3},{1,2},{2,1},{3,0},{4,7},{5,6},{6,5},{7,4},{8,11},{9,10},{10,... | collective-permute-start | bytes 786440 | tf_op jit(solution)/shard_map/ppermute | solution.py:576
  27.8 16.1 %collective-permute-start.39 = (bf16[2,64,2048]{2,1,0:T(8,128)(2,1)}, bf16[2,64,2048]{2,1,0:T(8,128)(2,1)S(1)}, u32[]{:S(2)}, u32[]{:S(2)}) collective-permute-start(bf16[2,64,2048]{2,1,0:T(8,128)(2,1)} %get-tuple-element.371), channel_id=1, source_target_pairs={{0,4},{1,5},{2,6},{3,7},{4,8},{5,9},{6,10},{7,11},{8,12},{9,13},{1... | collective-permute-start | bytes 1572872 | tf_op jit(solution)/shard_map/ppermute | solution.py:597
  31.4 17.0 %collective-permute-start.40 = (bf16[2,64,2048]{2,1,0:T(8,128)(2,1)}, bf16[2,64,2048]{2,1,0:T(8,128)(2,1)}, u32[]{:S(2)}, u32[]{:S(2)}) collective-permute-start(bf16[2,64,2048]{2,1,0:T(8,128)(2,1)} %get-tuple-element.372), channel_id=1, source_target_pairs={{4,0},{5,1},{6,2},{7,3},{8,4},{9,5},{10,6},{11,7},{12,8},{13,9},{1... | collective-permute-start | bytes 1572872 | tf_op jit(solution)/shard_map/ppermute | solution.py:598
  38.0 17.9 %collective-permute-start.48 = (bf16[2,64,2048]{2,1,0:T(8,128)(2,1)}, bf16[2,64,2048]{2,1,0:T(8,128)(2,1)S(1)}, u32[]{:S(2)}, u32[]{:S(2)}) collective-permute-start(bf16[2,64,2048]{2,1,0:T(8,128)(2,1)} %get-tuple-element.399), channel_id=1, source_target_pairs={{0,4},{1,5},{2,6},{3,7},{4,8},{5,9},{6,10},{7,11},{8,12},{9,13},{1... | collective-permute-start | bytes 1572872 | tf_op jit(solution)/shard_map/ppermute | solution.py:597
  41.5 18.1 %collective-permute-start.49 = (bf16[2,64,2048]{2,1,0:T(8,128)(2,1)}, bf16[2,64,2048]{2,1,0:T(8,128)(2,1)}, u32[]{:S(2)}, u32[]{:S(2)}) collective-permute-start(bf16[2,64,2048]{2,1,0:T(8,128)(2,1)} %get-tuple-element.400), channel_id=1, source_target_pairs={{4,0},{5,1},{6,2},{7,3},{8,4},{9,5},{10,6},{11,7},{12,8},{13,9},{1... | collective-permute-start | bytes 1572872 | tf_op jit(solution)/shard_map/ppermute | solution.py:598
  50.3 51.7 %collective-permute-start.41 = (bf16[2,64,2048]{2,1,0:T(8,128)(2,1)}, bf16[2,64,2048]{2,1,0:T(8,128)(2,1)}, u32[]{:S(2)}, u32[]{:S(2)}) collective-permute-start(bf16[2,64,2048]{2,1,0:T(8,128)(2,1)} %get-tuple-element.373), channel_id=1, source_target_pairs={{0,4},{1,5},{2,6},{3,7},{4,8},{5,9},{6,10},{7,11},{8,12},{9,13},{1... | collective-permute-start | bytes 1572872 | tf_op jit(solution)/shard_map/ppermute | solution.py:597
  54.6 47.4 %collective-permute-start.42 = (bf16[2,64,2048]{2,1,0:T(8,128)(2,1)}, bf16[2,64,2048]{2,1,0:T(8,128)(2,1)}, u32[]{:S(2)}, u32[]{:S(2)}) collective-permute-start(bf16[2,64,2048]{2,1,0:T(8,128)(2,1)} %get-tuple-element.374), channel_id=1, source_target_pairs={{4,0},{5,1},{6,2},{7,3},{8,4},{9,5},{10,6},{11,7},{12,8},{13,9},{1... | collective-permute-start | bytes 1572872 | tf_op jit(solution)/shard_map/ppermute | solution.py:598
  61.6 40.4 %collective-permute-start.50 = (bf16[2,64,2048]{2,1,0:T(8,128)(2,1)}, bf16[2,64,2048]{2,1,0:T(8,128)(2,1)}, u32[]{:S(2)}, u32[]{:S(2)}) collective-permute-start(bf16[2,64,2048]{2,1,0:T(8,128)(2,1)} %get-tuple-element.401), channel_id=1, source_target_pairs={{0,4},{1,5},{2,6},{3,7},{4,8},{5,9},{6,10},{7,11},{8,12},{9,13},{1... | collective-permute-start | bytes 1572872 | tf_op jit(solution)/shard_map/ppermute | solution.py:597
  65.9 36.1 %collective-permute-start.51 = (bf16[2,64,2048]{2,1,0:T(8,128)(2,1)}, bf16[2,64,2048]{2,1,0:T(8,128)(2,1)}, u32[]{:S(2)}, u32[]{:S(2)}) collective-permute-start(bf16[2,64,2048]{2,1,0:T(8,128)(2,1)} %get-tuple-element.402), channel_id=1, source_target_pairs={{4,0},{5,1},{6,2},{7,3},{8,4},{9,5},{10,6},{11,7},{12,8},{13,9},{1... | collective-permute-start | bytes 1572872 | tf_op jit(solution)/shard_map/ppermute | solution.py:598
  67.2 2.5 %collective-permute-start.46 = (bf16[1,32,2048]{2,1,0:T(8,128)(2,1)}, bf16[1,32,2048]{2,1,0:T(8,128)(2,1)S(1)}, u32[]{:S(2)}, u32[]{:S(2)}) collective-permute-start(bf16[1,32,2048]{2,1,0:T(8,128)(2,1)} %get-tuple-element.381), channel_id=1, source_target_pairs={{0,1},{1,2},{2,3},{3,4},{4,5},{5,6},{6,7},{7,8},{8,9},{9,10},{10,1... | collective-permute-start | bytes 393224 | tf_op jit(solution)/shard_map/ppermute | solution.py:604
  69.6 32.3 %collective-permute-start.47 = (bf16[1,32,2048]{2,1,0:T(8,128)(2,1)}, bf16[1,32,2048]{2,1,0:T(8,128)(2,1)S(1)}, u32[]{:S(2)}, u32[]{:S(2)}) collective-permute-start(bf16[1,32,2048]{2,1,0:T(8,128)(2,1)} %get-tuple-element.382), channel_id=1, source_target_pairs={{1,0},{2,1},{3,2},{4,3},{5,4},{6,5},{7,6},{8,7},{9,8},{10,9},{11,1... | collective-permute-start | bytes 393224 | tf_op jit(solution)/shard_map/ppermute | solution.py:605
  71.6 28.9 %all-to-all-start = ((bf16[16,16,128]{2,1,0:T(8,128)(2,1)}), bf16[16,16,128]{2,1,0:T(8,128)(2,1)S(1)}, u32[]{:S(2)}, u32[]{:S(2)}) async-start(bf16[16,16,128]{2,1,0:T(8,128)(2,1)} %tile.8), calls=%async_computation | async-start | bytes 131072 | tf_op jit(solution)/shard_map/all_to_all | solution.py:607
  100.5 0.6 copy-start.13
  102.0 42.3 %copy-start.14 = (bf16[16,32]{1,0:T(8,128)(2,1)S(1)}, bf16[16,32]{1,0:T(8,128)(2,1)}, u32[]{:S(2)}) copy-start(bf16[16,32]{1,0:T(8,128)(2,1)} %get-tuple-element.179.weight_ref) | copy-start | bytes 3076 | tf_op jit(solution)/shard_map/cond
  104.0 17.1 %collective-permute-start = (bf16[2,64,2048]{2,1,0:T(8,128)(2,1)}, bf16[2,64,2048]{2,1,0:T(8,128)(2,1)}, u32[]{:S(2)}, u32[]{:S(2)}) collective-permute-start(bf16[2,64,2048]{2,1,0:T(8,128)(2,1)} %get-tuple-element.190), channel_id=1, source_target_pairs={{0,4},{1,5},{2,6},{3,7},{4,8},{5,9},{6,10},{7,11},{8,12},{9,13},{1... | collective-permute-start | bytes 1572872 | tf_op jit(solution)/shard_map/cond/branch_0_fun/ppermute | solution.py:597
  109.4 17.0 %collective-permute-start.1 = (bf16[2,64,2048]{2,1,0:T(8,128)(2,1)}, bf16[2,64,2048]{2,1,0:T(8,128)(2,1)}, u32[]{:S(2)}, u32[]{:S(2)}) collective-permute-start(bf16[2,64,2048]{2,1,0:T(8,128)(2,1)} %get-tuple-element.191), channel_id=1, source_target_pairs={{4,0},{5,1},{6,2},{7,3},{8,4},{9,5},{10,6},{11,7},{12,8},{13,9},{1... | collective-permute-start | bytes 1572872 | tf_op jit(solution)/shard_map/cond/branch_0_fun/ppermute | solution.py:598
  112.6 31.7 %copy-start.2 = (f32[8,2,3,128,128]{4,3,2,1,0:T(8,128)S(1)}, f32[8,2,3,128,128]{4,3,2,1,0:T(8,128)}, u32[]{:S(2)}) copy-start(f32[8,2,3,128,128]{4,3,2,1,0:T(8,128)} %get-tuple-element.176.coef_ref) | copy-start | bytes 9437188 | tf_op jit(solution)/shard_map/cond
  112.6 30.7 %collective-permute-start.2 = (bf16[2,64,2048]{2,1,0:T(8,128)(2,1)}, bf16[2,64,2048]{2,1,0:T(8,128)(2,1)S(1)}, u32[]{:S(2)}, u32[]{:S(2)}) collective-permute-start(bf16[2,64,2048]{2,1,0:T(8,128)(2,1)} %get-tuple-element.201), channel_id=1, source_target_pairs={{0,4},{1,5},{2,6},{3,7},{4,8},{5,9},{6,10},{7,11},{8,12},{9,13},{1... | collective-permute-start | bytes 1572872 | tf_op jit(solution)/shard_map/cond/branch_0_fun/ppermute | solution.py:597
  118.3 25.1 %collective-permute-start.3 = (bf16[2,64,2048]{2,1,0:T(8,128)(2,1)}, bf16[2,64,2048]{2,1,0:T(8,128)(2,1)S(1)}, u32[]{:S(2)}, u32[]{:S(2)}) collective-permute-start(bf16[2,64,2048]{2,1,0:T(8,128)(2,1)} %get-tuple-element.202), channel_id=1, source_target_pairs={{4,0},{5,1},{6,2},{7,3},{8,4},{9,5},{10,6},{11,7},{12,8},{13,9},{1... | collective-permute-start | bytes 1572872 | tf_op jit(solution)/shard_map/cond/branch_0_fun/ppermute | solution.py:598
  143.3 0.8 copy-start.10
  143.3 1.0 copy-start.12
where the time goes:
time: 162 us; the launch traced here: 161 us
  Pallas kernels  60.8 us (38%)
  starting transfers between devices  58.5 us (36%)
  waiting for transfers between devices  29.5 us (18%)
  local copies, waits for them, and re-layouts  8.8 us (5%)
  between operations  2.43 us (2%)
    pallas_call x2, Pallas kernels, update(): pl.pallas_call(functools.partial(update_kernel, dense, part), grid_spec=p...  33.3 us
    ppermute x6, starting transfers between devices, run_slots(): ups[part].append(lax.ppermute(go_up, 'slab', ups_of(classes)))  26.6 us
    all_to_all x1, starting transfers between devices, on_device(): lax.all_to_all(ends, 'slab', split_axis=0, concat_axis=0, tiled=True)  16.6 us
    ppermute x6, waiting for transfers between devices, run_slots(): downs[part].append(lax.ppermute(go_down, 'slab', downs_of(classes)))  13.4 us
    ppermute x6, waiting for transfers between devices, on_device(): lax.ppermute(mine[d], 'slab', [(i, i ^ d) for i in range(nslab)])  12.2 us
    pallas_call x6, Pallas kernels, choose(): pl.pallas_call(functools.partial(choose_kernel, slot, part, len(up_from),...  11.6 us
    pallas_call x1, Pallas kernels, device_tables(): pl.pallas_call(functools.partial(tables_kernel, rows), grid_spec=pltpu.Pr...  8.94 us
    ppermute x6, starting transfers between devices, run_slots(): downs[part].append(lax.ppermute(go_down, 'slab', downs_of(classes)))  7.72 us
  transfers between devices with their start and end apart: 21, of which 9 were waited for; matrix products, arithmetic and copies ran while one was open for 3% of the time, Pallas kernels for 24%

commit v1 on v0

--- a/solution.py
+++ b/solution.py
@@ -564,17 +564,19 @@
         return update(volume, left, right, edge, tables, [seen], jnp.zeros((8, LANES), jnp.int32), None, 0, 1, True)[0]
 
     number = device.astype(jnp.int32)[None]
+    left = lax.ppermute(volume[slices - 1 :], "slab", ups_of(1))
+    right = lax.ppermute(volume[:1], "slab", downs_of(1))
     *runs, ends = turn(number, bases, measured[0], classes)
     row_of_bases = jnp.pad(bases, (0, LANES - angles), constant_values=1)[None]
     runs, row_of_bases = lax.optimization_barrier((runs, row_of_bases))
-    own = []
-    for part in range(PARTS):
+
+    def share_out(part):
         mine = [runs[d * PARTS + part] for d in range(classes)]
-        if part:
-            mine, own[-1] = lax.optimization_barrier((mine, own[-1]))
-        own.append(
-            mine[:1] + [lax.ppermute(mine[d], "slab", [(i, i ^ d) for i in range(nslab)]) for d in range(1, classes)]
-        )
+        return mine[:1] + [
+            lax.ppermute(mine[d], "slab", [(i, i ^ d) for i in range(nslab)]) for d in range(1, classes)
+        ]
+
+    own = [share_out(0)]
 
     most = -(-classes * (planes - 1) // LOAD) + planes - 2
     table = pl.pallas_call(
@@ -583,33 +585,32 @@
         out_shape=jax.ShapeDtypeStruct((16, LANES), jnp.int32),
         name="plan_slots",
     )(number, row_of_bases)
+    tables = device_tables(number, row_of_bases, fractions, path_weights, rows)
+    runs, own, table, tables, left, right = lax.optimization_barrier((runs, own, table, tables, left, right))
+    own += [share_out(part) for part in range(1, PARTS)]
     slots = table[PARTS * LINES, 0]
-    late = (ends, fractions, volume[slices - 1 :], volume[:1])
-
-    def run_slots(begin, end, ups, downs):
-        nonlocal late
+
+    def run_slots(begin, end, ups, downs, ends=None):
+        nonlocal table
         ups, downs = [list(u) for u in ups], [list(d) for d in downs]
+        edge = None
         for slot in range(begin, end):
             for part in range(PARTS):
                 go_up, go_down = choose(slot, part, table, own[part], ups[part], downs[part])
                 if slot == 0 and part == PARTS - 1:
-                    go_up, *late = lax.optimization_barrier((go_up, *late))
+                    go_up, ends = lax.optimization_barrier((go_up, ends))
+                    ends = jnp.tile(ends.astype(jnp.bfloat16)[None], (planes, 1, 1)).reshape(angles, cols // LANES, LANES)
+                    edge = lax.all_to_all(ends, "slab", split_axis=0, concat_axis=0, tiled=True).reshape(angles, cols)
+                    table, edge = lax.optimization_barrier((table, edge))
                 ups[part].append(lax.ppermute(go_up, "slab", ups_of(classes)))
                 downs[part].append(lax.ppermute(go_down, "slab", downs_of(classes)))
-        return ups, downs
-
-    ups, downs = run_slots(0, STEADY, [[] for _ in range(PARTS)], [[] for _ in range(PARTS)])
-    ends, late_fractions, low, high = late
-    tables = device_tables(number, row_of_bases, late_fractions, path_weights, rows)
-    left = lax.ppermute(low, "slab", ups_of(1))
-    right = lax.ppermute(high, "slab", downs_of(1))
-    ends = jnp.tile(ends.astype(jnp.bfloat16)[None], (planes, 1, 1)).reshape(angles, cols // LANES, LANES)
-    edge = lax.all_to_all(ends, "slab", split_axis=0, concat_axis=0, tiled=True).reshape(angles, cols)
-    left, right, edge, tables = lax.optimization_barrier((left, right, edge, tables))
+        return ups, downs, edge
+
+    ups, downs, edge = run_slots(0, STEADY, [[] for _ in range(PARTS)], [[] for _ in range(PARTS)], ends)
 
     def finish(end):
         def branch(ups, downs):
-            ups, downs = run_slots(STEADY, end, ups, downs)
+            ups, downs, _ = run_slots(STEADY, end, ups, downs)
             out, carry = None, edge
             for part in range(PARTS):
                 packets = own[part] + ups[part] + downs[part]

time: 162 us -> 160 us (0.988)
  blocking collectives: 0 us -> 18.2 us
  starting transfers between devices: 58.5 us -> 45.4 us
  waiting for transfers between devices: 29.5 us -> 24.9 us
  local copies, waits for them, and re-layouts: 8.8 us -> 6.08 us
    all_to_all x0 -> x1, blocking collectives: none -> 18.2 us  [run_slots(): lax.all_to_all(ends, 'slab', split_axis=0, concat_axis=0, tiled=True)]
    all_to_all x1 -> x0, starting transfers between devices: 16.6 us -> none  [on_device(): lax.all_to_all(ends, 'slab', split_axis=0, concat_axis=0, tiled=True)]
    ppermute x8, waiting for transfers between devices: 13.3 us -> 4.85 us  [the longest x6 4.85 us: share_out(): lax.ppermute(mine[d], 'slab', [(i, i ^ d) for i in range(nslab)])]
    ppermute x8, starting transfers between devices: 7.6 us -> 11.7 us  [the longest x6 7.39 us: share_out(): lax.ppermute(mine[d], 'slab', [(i, i ^ d) for i in range(nslab)])]
    ppermute x6, waiting for transfers between devices: 2.76 us -> 6.84 us  [run_slots(): ups[part].append(lax.ppermute(go_up, 'slab', ups_of(classes)))]
    unnamed x7 -> x9, local copies, waits for them, and re-layouts: 3.71 us -> 2.27 us
  transfers between devices with their start and end apart: 21 -> 20, of which waited for: 9 -> 7; matrix products, arithmetic and copies ran while one was open for 3% -> 1% of each run, Pallas kernels for 24% -> 24%
where the time goes in v1:
time: 160 us; the launch traced here: 159 us
  Pallas kernels  61 us (38%)
  starting transfers between devices  45.4 us (28%)
  waiting for transfers between devices  24.9 us (16%)
  blocking collectives  18.2 us (11%)
  local copies, waits for them, and re-layouts  6.08 us (4%)
  between operations  2.43 us (2%)
    pallas_call x2, Pallas kernels, update(): pl.pallas_call(functools.partial(update_kernel, dense, part), grid_spec=p...  33.4 us
    ppermute x6, starting transfers between devices, run_slots(): ups[part].append(lax.ppermute(go_up, 'slab', ups_of(classes)))  26 us
    all_to_all x1, blocking collectives, run_slots(): lax.all_to_all(ends, 'slab', split_axis=0, concat_axis=0, tiled=True)  18.2 us
    ppermute x6, waiting for transfers between devices, run_slots(): downs[part].append(lax.ppermute(go_down, 'slab', downs_of(classes)))  13.2 us
    pallas_call x6, Pallas kernels, choose(): pl.pallas_call(functools.partial(choose_kernel, slot, part, len(up_from),...  11.7 us
    pallas_call x1, Pallas kernels, device_tables(): pl.pallas_call(functools.partial(tables_kernel, rows), grid_spec=pltpu.Pr...  8.93 us
    ppermute x6, starting transfers between devices, run_slots(): downs[part].append(lax.ppermute(go_down, 'slab', downs_of(classes)))  7.72 us
    ppermute x6, starting transfers between devices, share_out(): lax.ppermute(mine[d], 'slab', [(i, i ^ d) for i in range(nslab)])  7.39 us
  transfers between devices with their start and end apart: 20, of which 7 were waited for; matrix products, arithmetic and copies ran while one was open for 1% of the time, Pallas kernels for 24%

profile of v1, /device:TPU:0, one launch (start us, length us, event | category | flops | bytes accessed | tf_op | source)
XLA Modules:
  0.0 159.1 jit_solution(7276183937084389960)
XLA Ops:
  1.2 1.6 copy-done
  3.4 3.6 %turn_rows.1 = (bf16[64,2048]{1,0:T(8,128)(2,1)S(1)}, bf16[64,2048]{1,0:T(8,128)(2,1)S(1)}, bf16[64,2048]{1,0:T(8,128)(2,1)S(1)}, bf16[64,2048]{1,0:T(8,128)(2,1...) custom-call(s32[1]{0:T(128)} %bitcast.device_ref, ...), custom_call_target="tpu_custom_call" | custom-call | tf_op jit(solution)/shard_map/turn_rows/pallas_call | solution.py:412
  7.5 2.6 %collective-permute-start.37 = (bf16[64,2048]{1,0:T(8,128)(2,1)S(1)}, bf16[64,2048]{1,0:T(8,128)(2,1)S(1)}, u32[]{:S(2)}, u32[]{:S(2)}) collective-permute-start(bf16[64,2048]{1,0:T(8,128)(2,1)S(1)} %get-tuple-element.360), channel_id=1, source_target_pairs={{0,2},{1,3},{2,0},{3,1},{4,6},{5,7},{6,4},{7,5},{8,10},{9,11},{10,... | collective-permute-start | bytes 786440 | tf_op jit(solution)/shard_map/ppermute | solution.py:576
  11.1 1.3 collective-permute-start.40
  12.4 3.0 %collective-permute-start.39 = (bf16[1,32,2048]{2,1,0:T(8,128)(2,1)S(1)}, bf16[1,32,2048]{2,1,0:T(8,128)(2,1)S(1)}, u32[]{:S(2)}, u32[]{:S(2)}) collective-permute-start(bf16[1,32,2048]{2,1,0:T(8,128)(2,1)S(1)} %get-tuple-element.403), channel_id=1, source_target_pairs={{0,1},{1,2},{2,3},{3,4},{4,5},{5,6},{6,7},{7,8},{8,9},{9,10},{10,1... | collective-permute-start | bytes 393224 | tf_op jit(solution)/shard_map/ppermute | solution.py:567
  15.5 3.4 %plan_slots.1.table_ref = s32[16,128]{1,0:T(8,128)S(1)} custom-call(s32[1]{0:T(128)} %bitcast.device_ref, s32[1,128]{1,0:T(1,128)} %pad_bitcast_fusion.bases_ref), custom_call_target="tpu_custom_call" | custom-call | tf_op jit(solution)/shard_map/plan_slots/pallas_call | solution.py:582
  18.9 8.9 %make_tables.1 = (f32[8,2,3,128,128]{4,3,2,1,0:T(8,128)}, f32[3,16,128]{2,1,0:T(8,128)S(1)}, bf16[128,256]{1,0:T(8,128)(2,1)}, bf16[8,512,256]{2,1,0:T(8,128)(2,1)}, bf16[8,32,16]{2,1,0:T(8,128)(2,1)}) custom-call(s32[1]{0:T(128)} %bitcast.device_ref, s32[1,128]{1,0:T(1,128)} %pad_bitcast_fusion.bases_ref, f32[16,2048]{1,0:T(8,128)} %after_ref.1, ...), custom_call_target="tpu_custom_call" | custom-call | tf_op jit(solution)/shard_map/make_tables/pallas_call | solution.py:347
  27.9 1.4 collective-permute-start.41
  29.3 2.8 %collective-permute-start.42 = (bf16[64,2048]{1,0:T(8,128)(2,1)S(1)}, bf16[64,2048]{1,0:T(8,128)(2,1)S(1)}, u32[]{:S(2)}, u32[]{:S(2)}) collective-permute-start(bf16[64,2048]{1,0:T(8,128)(2,1)S(1)} %get-tuple-element.374), channel_id=1, source_target_pairs={{0,2},{1,3},{2,0},{3,1},{4,6},{5,7},{6,4},{7,5},{8,10},{9,11},{10,... | collective-permute-start | bytes 786440 | tf_op jit(solution)/shard_map/ppermute | solution.py:576
  32.1 1.9 %choose_packet.41 = (bf16[2,64,2048]{2,1,0:T(8,128)(2,1)}, bf16[2,64,2048]{2,1,0:T(8,128)(2,1)}) custom-call(s32[16,128]{1,0:T(8,128)S(1)} %plan_slots.1.table_ref, bf16[64,2048]{1,0:T(8,128)(2,1)S(1)} %get-tuple-element.380.refs_0_.refs_4_.refs_5_, bf16[64,2048]{1,0:T(8,128)(2,1)S(1)} %collective-permute-done.36.refs_1_.refs_5_.refs_6_, ...), custom_call_target="tpu_custom_call" | custom-call | bytes 2097152 | tf_op jit(solution)/shard_map/choose_packet/pallas_call | solution.py:524
  34.1 3.5 %collective-permute-start.44 = (bf16[2,64,2048]{2,1,0:T(8,128)(2,1)}, bf16[2,64,2048]{2,1,0:T(8,128)(2,1)S(1)}, u32[]{:S(2)}, u32[]{:S(2)}) collective-permute-start(bf16[2,64,2048]{2,1,0:T(8,128)(2,1)} %get-tuple-element.384), channel_id=1, source_target_pairs={{0,4},{1,5},{2,6},{3,7},{4,8},{5,9},{6,10},{7,11},{8,12},{9,13},{1... | collective-permute-start | bytes 1572872 | tf_op jit(solution)/shard_map/ppermute | solution.py:605
  37.6 1.3 collective-permute-start.45
  39.2 4.5 %collective-permute-done.43.refs_3_.refs_7_.refs_8_ = bf16[64,2048]{1,0:T(8,128)(2,1)S(1)} collective-permute-done((bf16[64,2048]{1,0:T(8,128)(2,1)S(1)}, bf16[64,2048]{1,0:T(8,128)(2,1)S(1)}, u32[]{:S(2)}, u32[]{:S(2)}) %collective-permute-start.43) | collective-permute-done | bytes 262176 | tf_op jit(solution)/shard_map/ppermute | solution.py:576
  43.7 1.9 %choose_packet.40 = (bf16[2,64,2048]{2,1,0:T(8,128)(2,1)}, bf16[2,64,2048]{2,1,0:T(8,128)(2,1)}) custom-call(s32[16,128]{1,0:T(8,128)S(1)} %plan_slots.1.table_ref, bf16[64,2048]{1,0:T(8,128)(2,1)S(1)} %get-tuple-element.372.refs_0_.refs_4_.refs_5_, bf16[64,2048]{1,0:T(8,128)(2,1)S(1)} %collective-permute-done.41.refs_1_.refs_5_.refs_6_, ...), custom_call_target="tpu_custom_call" | custom-call | bytes 2097152 | tf_op jit(solution)/shard_map/choose_packet/pallas_call | solution.py:524
  45.7 3.5 %collective-permute-start.48 = (bf16[2,64,2048]{2,1,0:T(8,128)(2,1)}, bf16[2,64,2048]{2,1,0:T(8,128)(2,1)S(1)}, u32[]{:S(2)}, u32[]{:S(2)}) collective-permute-start(bf16[2,64,2048]{2,1,0:T(8,128)(2,1)} %get-tuple-element.397), channel_id=1, source_target_pairs={{0,4},{1,5},{2,6},{3,7},{4,8},{5,9},{6,10},{7,11},{8,12},{9,13},{1... | collective-permute-start | bytes 1572872 | tf_op jit(solution)/shard_map/ppermute | solution.py:605
  50.6 18.2 %all_to_all.5 = bf16[16,16,128]{2,1,0:T(8,128)(2,1)S(1)} all-to-all(bf16[16,16,128]{2,1,0:T(8,128)(2,1)S(1)} %tile.8), channel_id=1, replica_groups=mesh['groups'=2,'slab'=16] {'slab'}, dimensions={0} | all-to-all | bytes 131072 | tf_op jit(solution)/shard_map/all_to_all | solution.py:603
  68.8 2.0 %choose_packet.42 = (bf16[2,64,2048]{2,1,0:T(8,128)(2,1)}, bf16[2,64,2048]{2,1,0:T(8,128)(2,1)}) custom-call(s32[16,128]{1,0:T(8,128)S(1)} %plan_slots.1.table_ref, bf16[64,2048]{1,0:T(8,128)(2,1)S(1)} %get-tuple-element.380.refs_0_.refs_4_.refs_5_, bf16[64,2048]{1,0:T(8,128)(2,1)S(1)} %collective-permute-done.36.refs_1_.refs_5_.refs_6_, ...), custom_call_target="tpu_custom_call" | custom-call | bytes 2097152 | tf_op jit(solution)/shard_map/choose_packet/pallas_call | solution.py:524
  70.8 4.2 %collective-permute-start.46 = (bf16[2,64,2048]{2,1,0:T(8,128)(2,1)}, bf16[2,64,2048]{2,1,0:T(8,128)(2,1)}, u32[]{:S(2)}, u32[]{:S(2)}) collective-permute-start(bf16[2,64,2048]{2,1,0:T(8,128)(2,1)} %get-tuple-element.386), channel_id=1, source_target_pairs={{0,4},{1,5},{2,6},{3,7},{4,8},{5,9},{6,10},{7,11},{8,12},{9,13},{1... | collective-permute-start | bytes 1572872 | tf_op jit(solution)/shard_map/ppermute | solution.py:605
  76.3 2.0 %choose_packet.43 = (bf16[2,64,2048]{2,1,0:T(8,128)(2,1)}, bf16[2,64,2048]{2,1,0:T(8,128)(2,1)}) custom-call(s32[16,128]{1,0:T(8,128)S(1)} %plan_slots.1.table_ref, bf16[64,2048]{1,0:T(8,128)(2,1)S(1)} %get-tuple-element.372.refs_0_.refs_4_.refs_5_, bf16[64,2048]{1,0:T(8,128)(2,1)S(1)} %collective-permute-done.41.refs_1_.refs_5_.refs_6_, ...), custom_call_target="tpu_custom_call" | custom-call | bytes 2097152 | tf_op jit(solution)/shard_map/choose_packet/pallas_call | solution.py:524
  78.3 6.1 %collective-permute-start.50 = (bf16[2,64,2048]{2,1,0:T(8,128)(2,1)}, bf16[2,64,2048]{2,1,0:T(8,128)(2,1)}, u32[]{:S(2)}, u32[]{:S(2)}) collective-permute-start(bf16[2,64,2048]{2,1,0:T(8,128)(2,1)} %get-tuple-element.399), channel_id=1, source_target_pairs={{0,4},{1,5},{2,6},{3,7},{4,8},{5,9},{6,10},{7,11},{8,12},{9,13},{1... | collective-permute-start | bytes 1572872 | tf_op jit(solution)/shard_map/ppermute | solution.py:605
  88.9 3.1 %collective-permute-done.47 = bf16[2,64,2048]{2,1,0:T(8,128)(2,1)} collective-permute-done((bf16[2,64,2048]{2,1,0:T(8,128)(2,1)}, bf16[2,64,2048]{2,1,0:T(8,128)(2,1)}, u32[]{:S(2)}, u32[]{:S(2)}) %collective-permute-start.47) | collective-permute-done | bytes 524320 | tf_op jit(solution)/shard_map/ppermute | solution.py:606
  92.0 5.1 %collective-permute-done.50 = bf16[2,64,2048]{2,1,0:T(8,128)(2,1)} collective-permute-done((bf16[2,64,2048]{2,1,0:T(8,128)(2,1)}, bf16[2,64,2048]{2,1,0:T(8,128)(2,1)}, u32[]{:S(2)}, u32[]{:S(2)}) %collective-permute-start.50) | collective-permute-done | bytes 524320 | tf_op jit(solution)/shard_map/ppermute | solution.py:605
  97.2 4.9 %collective-permute-done.51 = bf16[2,64,2048]{2,1,0:T(8,128)(2,1)} collective-permute-done((bf16[2,64,2048]{2,1,0:T(8,128)(2,1)}, bf16[2,64,2048]{2,1,0:T(8,128)(2,1)}, u32[]{:S(2)}, u32[]{:S(2)}) %collective-permute-start.51) | collective-permute-done | bytes 524320 | tf_op jit(solution)/shard_map/ppermute | solution.py:606
  102.1 56.8 %conditional.1 = (f32[128,32,2048]{2,1,0:T(8,128)}) conditional(s32[]{:T(128)} %clamp.3, (s32[16,128]{1,0:T(8,128)S(1)}, bf16[64,2048]{1,0:T(8,128)(2,1)S(1)}, bf16[64,2048]{1,0:T(8,128)(2,1)S(1)}, bf16[64,2048]{1,0:T(8,128)(2,1)S(1)}, bf16[64,2048]{1,0:T(8,128)(2,1)S(1)}, /*index=5*/bf16[2,64,2048]{2,1,0:T(8,128)(2,1)S(1)}, ...), branch_computations={%region_1.2_spmd, %region_2.3_spmd, %region_3.4_spmd} | conditional | flops 536870912 | bytes 152343712 | solution.py:624
  102.1 1.9 %choose_packet.22 = (bf16[2,64,2048]{2,1,0:T(8,128)(2,1)}, bf16[2,64,2048]{2,1,0:T(8,128)(2,1)}) custom-call(s32[16,128]{1,0:T(8,128)S(1)} %get-tuple-element.170.table_ref, bf16[64,2048]{1,0:T(8,128)(2,1)S(1)} %get-tuple-element.182.refs_0_.refs_6_.rest_0_, bf16[64,2048]{1,0:T(8,128)(2,1)S(1)} %get-tuple-element.183.refs_1_.refs_7_.rest_1_, ...), custom_call_target="tpu_custom_call" | custom-call | bytes 2097152 | tf_op jit(solution)/shard_map/cond/branch_0_fun/choose_packet/pallas_call | solution.py:524
  104.1 3.0 %collective-permute-start = (bf16[2,64,2048]{2,1,0:T(8,128)(2,1)}, bf16[2,64,2048]{2,1,0:T(8,128)(2,1)}, u32[]{:S(2)}, u32[]{:S(2)}) collective-permute-start(bf16[2,64,2048]{2,1,0:T(8,128)(2,1)} %get-tuple-element.190), channel_id=1, source_target_pairs={{0,4},{1,5},{2,6},{3,7},{4,8},{5,9},{6,10},{7,11},{8,12},{9,13},{1... | collective-permute-start | bytes 1572872 | tf_op jit(solution)/shard_map/cond/branch_0_fun/ppermute | solution.py:605
  108.4 2.0 %choose_packet.23 = (bf16[2,64,2048]{2,1,0:T(8,128)(2,1)}, bf16[2,64,2048]{2,1,0:T(8,128)(2,1)}) custom-call(s32[16,128]{1,0:T(8,128)S(1)} %get-tuple-element.170.table_ref, bf16[64,2048]{1,0:T(8,128)(2,1)S(1)} %get-tuple-element.193.refs_0_.refs_6_.rest_0_, bf16[64,2048]{1,0:T(8,128)(2,1)S(1)} %get-tuple-element.194.refs_1_.refs_7_.rest_1_, ...), custom_call_target="tpu_custom_call" | custom-call | bytes 2097152 | tf_op jit(solution)/shard_map/cond/branch_0_fun/choose_packet/pallas_call | solution.py:524
  110.4 5.6 %collective-permute-start.2 = (bf16[2,64,2048]{2,1,0:T(8,128)(2,1)}, bf16[2,64,2048]{2,1,0:T(8,128)(2,1)S(1)}, u32[]{:S(2)}, u32[]{:S(2)}) collective-permute-start(bf16[2,64,2048]{2,1,0:T(8,128)(2,1)} %get-tuple-element.201), channel_id=1, source_target_pairs={{0,4},{1,5},{2,6},{3,7},{4,8},{5,9},{6,10},{7,11},{8,12},{9,13},{1... | collective-permute-start | bytes 1572872 | tf_op jit(solution)/shard_map/cond/branch_0_fun/ppermute | solution.py:605
  117.3 1.7 %collective-permute-done.rest_6_ = bf16[2,64,2048]{2,1,0:T(8,128)(2,1)} collective-permute-done((bf16[2,64,2048]{2,1,0:T(8,128)(2,1)}, bf16[2,64,2048]{2,1,0:T(8,128)(2,1)}, u32[]{:S(2)}, u32[]{:S(2)}) %collective-permute-start) | collective-permute-done | bytes 524320 | tf_op jit(solution)/shard_map/cond/branch_0_fun/ppermute | solution.py:605
  119.0 5.2 %collective-permute-done.1.rest_9_ = bf16[2,64,2048]{2,1,0:T(8,128)(2,1)} collective-permute-done((bf16[2,64,2048]{2,1,0:T(8,128)(2,1)}, bf16[2,64,2048]{2,1,0:T(8,128)(2,1)}, u32[]{:S(2)}, u32[]{:S(2)}) %collective-permute-start.1) | collective-permute-done | bytes 524320 | tf_op jit(solution)/shard_map/cond/branch_0_fun/ppermute | solution.py:606
  124.1 16.9 %slab_update.6 = (f32[128,32,2048]{2,1,0:T(8,128)}, bf16[16,2048]{1,0:T(8,128)(2,1)}) custom-call(s32[16,128]{1,0:T(8,128)S(1)} %get-tuple-element.170.table_ref, bf16[128,32,2048]{2,1,0:T(8,128)(2,1)} %get-tuple-element.172.lower_ref.upper_ref.next_ref, bf16[128,32,2048]{2,1,0:T(8,128)(2,1)} %get-tuple-element.172.lower_ref.upper_ref.next_ref, ...), custom_call_target="tpu_custom_call" | custom-call | flops 268435456 | bytes 29360128 | tf_op jit(solution)/shard_map/cond/branch_0_fun/slab_update/pallas_call | solution.py:158
  142.1 16.5 %slab_update.7 = (f32[128,32,2048]{2,1,0:T(8,128)}, bf16[16,2048]{1,0:T(8,128)(2,1)}) custom-call(s32[16,128]{1,0:T(8,128)S(1)} %get-tuple-element.170.table_ref, bf16[128,32,2048]{2,1,0:T(8,128)(2,1)} %get-tuple-element.172.lower_ref.upper_ref.next_ref, ...), custom_call_target="tpu_custom_call", output_to_operand_aliasing={{0}: (23, {})} | custom-call | flops 268435456 | bytes 29360128 | tf_op jit(solution)/shard_map/cond/branch_0_fun/slab_update/pallas_call | solution.py:158
  (49 shorter events, 12.6 us)
Async XLA Ops:
  1.2 1.6 copy-start
  2.8 0.7 copy-start.1
  7.0 20.9 %collective-permute-start.36 = (bf16[64,2048]{1,0:T(8,128)(2,1)S(1)}, bf16[64,2048]{1,0:T(8,128)(2,1)S(1)}, u32[]{:S(2)}, u32[]{:S(2)}) collective-permute-start(bf16[64,2048]{1,0:T(8,128)(2,1)S(1)} %get-tuple-element.358), channel_id=1, source_target_pairs={{0,1},{1,0},{2,3},{3,2},{4,5},{5,4},{6,7},{7,6},{8,9},{9,8},{10,11... | collective-permute-start | bytes 786440 | tf_op jit(solution)/shard_map/ppermute | solution.py:576
  7.5 20.3 %collective-permute-start.37 = (bf16[64,2048]{1,0:T(8,128)(2,1)S(1)}, bf16[64,2048]{1,0:T(8,128)(2,1)S(1)}, u32[]{:S(2)}, u32[]{:S(2)}) collective-permute-start(bf16[64,2048]{1,0:T(8,128)(2,1)S(1)} %get-tuple-element.360), channel_id=1, source_target_pairs={{0,2},{1,3},{2,0},{3,1},{4,6},{5,7},{6,4},{7,5},{8,10},{9,11},{10,... | collective-permute-start | bytes 786440 | tf_op jit(solution)/shard_map/ppermute | solution.py:576
  10.1 17.8 %collective-permute-start.38 = (bf16[64,2048]{1,0:T(8,128)(2,1)S(1)}, bf16[64,2048]{1,0:T(8,128)(2,1)S(1)}, u32[]{:S(2)}, u32[]{:S(2)}) collective-permute-start(bf16[64,2048]{1,0:T(8,128)(2,1)S(1)} %get-tuple-element.362), channel_id=1, source_target_pairs={{0,3},{1,2},{2,1},{3,0},{4,7},{5,6},{6,5},{7,4},{8,11},{9,10},{10,... | collective-permute-start | bytes 786440 | tf_op jit(solution)/shard_map/ppermute | solution.py:576
  11.1 16.7 %collective-permute-start.40 = (bf16[1,32,2048]{2,1,0:T(8,128)(2,1)S(1)}, bf16[1,32,2048]{2,1,0:T(8,128)(2,1)S(1)}, u32[]{:S(2)}, u32[]{:S(2)}) collective-permute-start(bf16[1,32,2048]{2,1,0:T(8,128)(2,1)S(1)} %get-tuple-element.402), channel_id=1, source_target_pairs={{1,0},{2,1},{3,2},{4,3},{5,4},{6,5},{7,6},{8,7},{9,8},{10,9},{11,1... | collective-permute-start | bytes 393224 | tf_op jit(solution)/shard_map/ppermute | solution.py:568
  12.4 15.4 %collective-permute-start.39 = (bf16[1,32,2048]{2,1,0:T(8,128)(2,1)S(1)}, bf16[1,32,2048]{2,1,0:T(8,128)(2,1)S(1)}, u32[]{:S(2)}, u32[]{:S(2)}) collective-permute-start(bf16[1,32,2048]{2,1,0:T(8,128)(2,1)S(1)} %get-tuple-element.403), channel_id=1, source_target_pairs={{0,1},{1,2},{2,3},{3,4},{4,5},{5,6},{6,7},{7,8},{8,9},{9,10},{10,1... | collective-permute-start | bytes 393224 | tf_op jit(solution)/shard_map/ppermute | solution.py:567
  27.8 6.2 %copy-start.5 = (bf16[1,32,2048]{2,1,0:T(8,128)(2,1)}, bf16[1,32,2048]{2,1,0:T(8,128)(2,1)S(1)}, u32[]{:S(2)}) copy-start(bf16[1,32,2048]{2,1,0:T(8,128)(2,1)S(1)} %collective-permute-done.40) | copy-start | bytes 393220
  27.8 6.2 %copy-start.9 = (bf16[1,32,2048]{2,1,0:T(8,128)(2,1)}, bf16[1,32,2048]{2,1,0:T(8,128)(2,1)S(1)}, u32[]{:S(2)}) copy-start(bf16[1,32,2048]{2,1,0:T(8,128)(2,1)S(1)} %collective-permute-done.39) | copy-start | bytes 393220
  27.9 11.0 %collective-permute-start.41 = (bf16[64,2048]{1,0:T(8,128)(2,1)S(1)}, bf16[64,2048]{1,0:T(8,128)(2,1)S(1)}, u32[]{:S(2)}, u32[]{:S(2)}) collective-permute-start(bf16[64,2048]{1,0:T(8,128)(2,1)S(1)} %get-tuple-element.373), channel_id=1, source_target_pairs={{0,1},{1,0},{2,3},{3,2},{4,5},{5,4},{6,7},{7,6},{8,9},{9,8},{10,11... | collective-permute-start | bytes 786440 | tf_op jit(solution)/shard_map/ppermute | solution.py:576
  29.3 9.9 %collective-permute-start.42 = (bf16[64,2048]{1,0:T(8,128)(2,1)S(1)}, bf16[64,2048]{1,0:T(8,128)(2,1)S(1)}, u32[]{:S(2)}, u32[]{:S(2)}) collective-permute-start(bf16[64,2048]{1,0:T(8,128)(2,1)S(1)} %get-tuple-element.374), channel_id=1, source_target_pairs={{0,2},{1,3},{2,0},{3,1},{4,6},{5,7},{6,4},{7,5},{8,10},{9,11},{10,... | collective-permute-start | bytes 786440 | tf_op jit(solution)/shard_map/ppermute | solution.py:576
  32.1 11.6 %collective-permute-start.43 = (bf16[64,2048]{1,0:T(8,128)(2,1)S(1)}, bf16[64,2048]{1,0:T(8,128)(2,1)S(1)}, u32[]{:S(2)}, u32[]{:S(2)}) collective-permute-start(bf16[64,2048]{1,0:T(8,128)(2,1)S(1)} %get-tuple-element.375), channel_id=1, source_target_pairs={{0,3},{1,2},{2,1},{3,0},{4,7},{5,6},{6,5},{7,4},{8,11},{9,10},{10,... | collective-permute-start | bytes 786440 | tf_op jit(solution)/shard_map/ppermute | solution.py:576
  34.1 34.7 %collective-permute-start.44 = (bf16[2,64,2048]{2,1,0:T(8,128)(2,1)}, bf16[2,64,2048]{2,1,0:T(8,128)(2,1)S(1)}, u32[]{:S(2)}, u32[]{:S(2)}) collective-permute-start(bf16[2,64,2048]{2,1,0:T(8,128)(2,1)} %get-tuple-element.384), channel_id=1, source_target_pairs={{0,4},{1,5},{2,6},{3,7},{4,8},{5,9},{6,10},{7,11},{8,12},{9,13},{1... | collective-permute-start | bytes 1572872 | tf_op jit(solution)/shard_map/ppermute | solution.py:605
  37.6 31.2 %collective-permute-start.45 = (bf16[2,64,2048]{2,1,0:T(8,128)(2,1)}, bf16[2,64,2048]{2,1,0:T(8,128)(2,1)}, u32[]{:S(2)}, u32[]{:S(2)}) collective-permute-start(bf16[2,64,2048]{2,1,0:T(8,128)(2,1)} %get-tuple-element.385), channel_id=1, source_target_pairs={{4,0},{5,1},{6,2},{7,3},{8,4},{9,5},{10,6},{11,7},{12,8},{13,9},{1... | collective-permute-start | bytes 1572872 | tf_op jit(solution)/shard_map/ppermute | solution.py:606
  45.7 30.6 %collective-permute-start.48 = (bf16[2,64,2048]{2,1,0:T(8,128)(2,1)}, bf16[2,64,2048]{2,1,0:T(8,128)(2,1)S(1)}, u32[]{:S(2)}, u32[]{:S(2)}) collective-permute-start(bf16[2,64,2048]{2,1,0:T(8,128)(2,1)} %get-tuple-element.397), channel_id=1, source_target_pairs={{0,4},{1,5},{2,6},{3,7},{4,8},{5,9},{6,10},{7,11},{8,12},{9,13},{1... | collective-permute-start | bytes 1572872 | tf_op jit(solution)/shard_map/ppermute | solution.py:605
  49.2 27.1 %collective-permute-start.49 = (bf16[2,64,2048]{2,1,0:T(8,128)(2,1)}, bf16[2,64,2048]{2,1,0:T(8,128)(2,1)}, u32[]{:S(2)}, u32[]{:S(2)}) collective-permute-start(bf16[2,64,2048]{2,1,0:T(8,128)(2,1)} %get-tuple-element.398), channel_id=1, source_target_pairs={{4,0},{5,1},{6,2},{7,3},{8,4},{9,5},{10,6},{11,7},{12,8},{13,9},{1... | collective-permute-start | bytes 1572872 | tf_op jit(solution)/shard_map/ppermute | solution.py:606
  70.8 18.1 %collective-permute-start.46 = (bf16[2,64,2048]{2,1,0:T(8,128)(2,1)}, bf16[2,64,2048]{2,1,0:T(8,128)(2,1)}, u32[]{:S(2)}, u32[]{:S(2)}) collective-permute-start(bf16[2,64,2048]{2,1,0:T(8,128)(2,1)} %get-tuple-element.386), channel_id=1, source_target_pairs={{0,4},{1,5},{2,6},{3,7},{4,8},{5,9},{6,10},{7,11},{8,12},{9,13},{1... | collective-permute-start | bytes 1572872 | tf_op jit(solution)/shard_map/ppermute | solution.py:605
  75.0 17.0 %collective-permute-start.47 = (bf16[2,64,2048]{2,1,0:T(8,128)(2,1)}, bf16[2,64,2048]{2,1,0:T(8,128)(2,1)}, u32[]{:S(2)}, u32[]{:S(2)}) collective-permute-start(bf16[2,64,2048]{2,1,0:T(8,128)(2,1)} %get-tuple-element.387), channel_id=1, source_target_pairs={{4,0},{5,1},{6,2},{7,3},{8,4},{9,5},{10,6},{11,7},{12,8},{13,9},{1... | collective-permute-start | bytes 1572872 | tf_op jit(solution)/shard_map/ppermute | solution.py:606
  78.3 18.9 %collective-permute-start.50 = (bf16[2,64,2048]{2,1,0:T(8,128)(2,1)}, bf16[2,64,2048]{2,1,0:T(8,128)(2,1)}, u32[]{:S(2)}, u32[]{:S(2)}) collective-permute-start(bf16[2,64,2048]{2,1,0:T(8,128)(2,1)} %get-tuple-element.399), channel_id=1, source_target_pairs={{0,4},{1,5},{2,6},{3,7},{4,8},{5,9},{6,10},{7,11},{8,12},{9,13},{1... | collective-permute-start | bytes 1572872 | tf_op jit(solution)/shard_map/ppermute | solution.py:605
  84.4 17.7 %collective-permute-start.51 = (bf16[2,64,2048]{2,1,0:T(8,128)(2,1)}, bf16[2,64,2048]{2,1,0:T(8,128)(2,1)}, u32[]{:S(2)}, u32[]{:S(2)}) collective-permute-start(bf16[2,64,2048]{2,1,0:T(8,128)(2,1)} %get-tuple-element.400), channel_id=1, source_target_pairs={{4,0},{5,1},{6,2},{7,3},{8,4},{9,5},{10,6},{11,7},{12,8},{13,9},{1... | collective-permute-start | bytes 1572872 | tf_op jit(solution)/shard_map/ppermute | solution.py:606
  102.1 39.9 %copy-start.6 = (bf16[1,32,2048]{2,1,0:T(8,128)(2,1)S(1)}, bf16[1,32,2048]{2,1,0:T(8,128)(2,1)}, u32[]{:S(2)}) copy-start(bf16[1,32,2048]{2,1,0:T(8,128)(2,1)} %get-tuple-element.174.right_ref) | copy-start | bytes 393220 | tf_op jit(solution)/shard_map/cond
  102.1 40.0 %copy-start.10 = (bf16[1,32,2048]{2,1,0:T(8,128)(2,1)S(1)}, bf16[1,32,2048]{2,1,0:T(8,128)(2,1)}, u32[]{:S(2)}) copy-start(bf16[1,32,2048]{2,1,0:T(8,128)(2,1)} %get-tuple-element.173.left_ref) | copy-start | bytes 393220 | tf_op jit(solution)/shard_map/cond
  102.1 40.0 %copy-start.21 = (bf16[16,32]{1,0:T(8,128)(2,1)S(1)}, bf16[16,32]{1,0:T(8,128)(2,1)}, u32[]{:S(2)}) copy-start(bf16[16,32]{1,0:T(8,128)(2,1)} %get-tuple-element.179.weight_ref) | copy-start | bytes 3076 | tf_op jit(solution)/shard_map/cond
  104.1 14.9 %collective-permute-start = (bf16[2,64,2048]{2,1,0:T(8,128)(2,1)}, bf16[2,64,2048]{2,1,0:T(8,128)(2,1)}, u32[]{:S(2)}, u32[]{:S(2)}) collective-permute-start(bf16[2,64,2048]{2,1,0:T(8,128)(2,1)} %get-tuple-element.190), channel_id=1, source_target_pairs={{0,4},{1,5},{2,6},{3,7},{4,8},{5,9},{6,10},{7,11},{8,12},{9,13},{1... | collective-permute-start | bytes 1572872 | tf_op jit(solution)/shard_map/cond/branch_0_fun/ppermute | solution.py:605
  107.1 17.1 %collective-permute-start.1 = (bf16[2,64,2048]{2,1,0:T(8,128)(2,1)}, bf16[2,64,2048]{2,1,0:T(8,128)(2,1)}, u32[]{:S(2)}, u32[]{:S(2)}) collective-permute-start(bf16[2,64,2048]{2,1,0:T(8,128)(2,1)} %get-tuple-element.191), channel_id=1, source_target_pairs={{4,0},{5,1},{6,2},{7,3},{8,4},{9,5},{10,6},{11,7},{12,8},{13,9},{1... | collective-permute-start | bytes 1572872 | tf_op jit(solution)/shard_map/cond/branch_0_fun/ppermute | solution.py:606
  110.3 31.7 %copy-start.2 = (f32[8,2,3,128,128]{4,3,2,1,0:T(8,128)S(1)}, f32[8,2,3,128,128]{4,3,2,1,0:T(8,128)}, u32[]{:S(2)}) copy-start(f32[8,2,3,128,128]{4,3,2,1,0:T(8,128)} %get-tuple-element.176.coef_ref) | copy-start | bytes 9437188 | tf_op jit(solution)/shard_map/cond
  110.4 30.7 %collective-permute-start.2 = (bf16[2,64,2048]{2,1,0:T(8,128)(2,1)}, bf16[2,64,2048]{2,1,0:T(8,128)(2,1)S(1)}, u32[]{:S(2)}, u32[]{:S(2)}) collective-permute-start(bf16[2,64,2048]{2,1,0:T(8,128)(2,1)} %get-tuple-element.201), channel_id=1, source_target_pairs={{0,4},{1,5},{2,6},{3,7},{4,8},{5,9},{6,10},{7,11},{8,12},{9,13},{1... | collective-permute-start | bytes 1572872 | tf_op jit(solution)/shard_map/cond/branch_0_fun/ppermute | solution.py:605
  116.0 25.1 %collective-permute-start.3 = (bf16[2,64,2048]{2,1,0:T(8,128)(2,1)}, bf16[2,64,2048]{2,1,0:T(8,128)(2,1)S(1)}, u32[]{:S(2)}, u32[]{:S(2)}) collective-permute-start(bf16[2,64,2048]{2,1,0:T(8,128)(2,1)} %get-tuple-element.202), channel_id=1, source_target_pairs={{4,0},{5,1},{6,2},{7,3},{8,4},{9,5},{10,6},{11,7},{12,8},{13,9},{1... | collective-permute-start | bytes 1572872 | tf_op jit(solution)/shard_map/cond/branch_0_fun/ppermute | solution.py:606
  141.1 0.8 copy-start.18
  141.1 1.0 copy-start.20
